TPU v7x, 256 devices: a whole 4x4x8 slice. The times are simulated.
256 devices in a mesh: space: 32 (over z_lo, x, core), mode: 8 (over y, z_hi).
Axes of the slice: x: 4, y: 4, z: 8 (z_hi: 2, z_lo: 4; z = z_hi * 4 + z_lo), core: 2. Of those that a mesh axis runs over, the one named last changes fastest.
Arguments:
- pressure: float32 [56, 256, 32, 128], P('mode', 'space'), may hold values from -0.3 to 0.3
- source: float32 [56, 256, 32, 128], P('mode', 'space'), may hold values from -4 to 4
- kl_field: float32 [6, 256, 32, 128], P(None, 'space'), may hold values from -3 to 10, as said below
- coupling_list: int32 [4, 210], replicated, may hold values from 0 to 55, as said below
Outputs:
- correction: float32 [56, 256, 32, 128], P('mode', 'space')
- residual: float32 [56, 256, 32, 128], P('mode', 'space')
Inputs may be any that keep to these rules, and one draw needn't show every extreme that they name: Column n states that mode coupling_list[0, n] couples to mode coupling_list[1, n] through field coupling_list[2, n], from 1 to 5, with the weight sqrt(coupling_list[3, n]), the code running from 1 to 3. The columns are all couplings of the normalized Hermite chaos of total degree 3 in 5 variables, each once, under a numbering of the 56 modes and an order of the columns drawn from the seed; with (i, j, k, code) the list also holds (j, i, k, code). kl_field[0], the mean permeability, lies between 1 and 10; the fields 1 to 5 lie between -3 and 3.
All inputs are finite; a program needn't handle non-finite values.
Results may differ from a plain program's by a relative error of at most 0.0003.
Values sent between devices are 32-bit elements; how exact they have to be, the bound alone decides.
A program may use at most 128 MiB of HBM per device.

v0:
```python
import jax
import jax.numpy as jnp
from jax import lax
from jax.sharding import PartitionSpec as P

P_SIZE = 56
KL = 5
SWEEPS = 2
COARSE = 8
LEVELS = 4


damping = 0.8


def padded(cells, sides, width):
    for axis, dim in sides:
        count = lax.axis_size(axis)
        ends = count - 1
        head = lax.slice_in_dim(cells, 0, width, axis=dim)
        tail = lax.slice_in_dim(cells, cells.shape[dim] - width, cells.shape[dim], axis=dim)
        cells = jnp.concatenate(
            [
                lax.ppermute(tail, axis, [(i, (i + 1) % count) for i in range(ends)]),
                cells,
                lax.ppermute(head, axis, [((i + 1) % count, i) for i in range(ends)]),
            ],
            axis=dim,
        )
    return cells


def along_last(values, offset):
    size = values.shape[-1]
    zeros = jnp.zeros(values.shape[:-1] + (abs(offset),), values.dtype)
    if offset > 0:
        return jnp.concatenate([values[..., offset:], zeros], axis=-1)
    return jnp.concatenate([zeros, values[..., : size + offset]], axis=-1)


def neighbours(values_rim, depth):
    values = values_rim[..., 1:-1, :]
    positions = lax.iota(jnp.int32, values.shape[-1]) % depth
    upper = positions < depth - 1
    lower = positions > 0
    others = (
        values_rim[..., 2:, :],
        values_rim[..., :-2, :],
        along_last(values, depth),
        along_last(values, -depth),
        jnp.where(upper, along_last(values, 1), 0.0),
        jnp.where(lower, along_last(values, -1), 0.0),
    )
    return (values, others)


def faces_of(field_rim, depth):
    field, others = neighbours(field_rim, depth)
    plane = field.shape[-1]
    places = lax.iota(jnp.int32, plane)
    within = places % depth
    inside = (places < plane - depth, places >= depth, within < depth - 1, within > 0)
    collected = [0.5 * (field + others[0]), 0.5 * (field + others[1])]
    for keep, other in zip(inside, others[2:]):
        collected.append(jnp.where(keep, 0.5 * (field + other), 0.0))
    return collected


def apply_operator(faces, values_rim, scale, depth):
    values, others = neighbours(values_rim, depth)
    total = faces[0] * (values - others[0])
    for face, other in zip(faces[1:], others[1:]):
        total = total + face * (values - other)
    return scale * total


def diagonal_of(faces, scale):
    total = faces[0]
    for face in faces[1:]:
        total = total + face
    return scale * total


def zero_rims(values):
    return jnp.pad(values, [(0, 0)] * (values.ndim - 2) + [(1, 1), (0, 0)])


def pair_yz(values, rows, depth):
    leading = values.shape[:-2]
    width = values.shape[-2]
    cells = values.reshape(leading + (width, rows, depth))
    cells = cells[..., 0::2] + cells[..., 1::2]
    cells = cells[..., 0::2, :] + cells[..., 1::2, :]
    return cells.reshape(leading + (width, rows // 2 * (depth // 2)))


def pair_x(values):
    return values[..., 0::2, :] + values[..., 1::2, :]


def restrict(values, rows, depth):
    return 0.125 * pair_x(pair_yz(values, rows, depth))


def prolong(values, rows, depth):
    leading = values.shape[:-2]
    width = values.shape[-2]
    cells = values.reshape(leading + (width, rows, depth))
    cells = jnp.repeat(jnp.repeat(cells, 2, axis=-1), 2, axis=-2)
    cells = cells.reshape(leading + (width, 4 * rows * depth))
    cells = jnp.repeat(cells, 2, axis=-2)
    return cells


def line_solve(faces, rest, scale):
    upper = scale * jnp.sum(faces[0], axis=-1)[0]
    lower = scale * jnp.sum(faces[1], axis=-1)[0]
    count = upper.shape[0]
    places = jnp.arange(count, dtype=jnp.int32)
    above = jnp.where(places < count - 1, -upper, jnp.zeros_like(upper))
    below = jnp.where(places > 0, -lower, jnp.zeros_like(lower))
    middle = upper + lower
    right = jnp.transpose(jnp.sum(rest, axis=-1))
    solved = lax.linalg.tridiagonal_solve(below, middle, above, right)
    return jnp.transpose(solved)[:, :, None]


def smooth(correction, residual, faces, diagonal, scale, depth, margin):
    return (
        correction
        + damping * (residual - apply_operator(faces, margin(correction), scale, depth)) / diagonal
    )


def fine_margin(values):
    return padded(values, (("space", 1),), 1)


def cycle(residual, field, level, rows, depth):
    scale = 0.25**level
    faces = faces_of(zero_rims(field), depth)
    diagonal = diagonal_of(faces, scale)
    correction = damping * residual / diagonal
    if level == LEVELS - 1:
        for turn in range(COARSE - 1):
            correction = smooth(correction, residual, faces, diagonal, scale, depth, zero_rims)
        rest = residual - apply_operator(faces, zero_rims(correction), scale, depth)
        return correction + line_solve(faces, rest, scale)
    correction = smooth(correction, residual, faces, diagonal, scale, depth, zero_rims)
    rest = residual - apply_operator(faces, zero_rims(correction), scale, depth)
    deeper = cycle(
        restrict(rest, rows, depth), restrict(field, rows, depth), level + 1, rows // 2, depth // 2
    )
    correction = correction + prolong(deeper, rows // 2, depth // 2)
    for turn in range(SWEEPS):
        correction = smooth(correction, residual, faces, diagonal, scale, depth, zero_rims)
    return correction


def coupling_tables(coupling_list):
    modes = jnp.arange(P_SIZE, dtype=jnp.int32)
    orders = jnp.arange(1, KL + 1, dtype=jnp.int32)
    firsts = (coupling_list[0][:, None] == modes[None, :]).astype(jnp.float32)
    seconds = (coupling_list[1][:, None] == modes[None, :]).astype(jnp.float32)
    weights = jnp.sqrt(coupling_list[3].astype(jnp.float32))
    which = (coupling_list[2][:, None] == orders[None, :]).astype(jnp.float32) * weights[:, None]
    return jnp.einsum("nk,ni,nj->kij", which, firsts, seconds, precision=lax.Precision.HIGHEST)


def local(pressure, source, kl_field, coupling_list):
    local_modes, width, rows, depth = pressure.shape
    plane = rows * depth
    pressure = pressure.reshape(local_modes, width, plane)
    source = source.reshape(local_modes, width, plane)
    fields = kl_field.reshape(kl_field.shape[0], width, plane)
    joined = padded(jnp.concatenate([pressure, fields], axis=0), (("space", 1),), 1)
    pressure_rim = joined[:local_modes]
    field_rim = joined[local_modes:]
    mean_faces = faces_of(field_rim[0:1], depth)
    spread_faces = faces_of(field_rim[1:, None], depth)
    image = apply_operator(mean_faces, pressure_rim, 1.0, depth)
    tables = coupling_tables(coupling_list)
    first = lax.axis_index("mode") * local_modes
    own_rows = lax.dynamic_slice_in_dim(tables, first, local_modes, axis=1)
    mixed = jnp.einsum(
        "kij,jxn->kixn",
        own_rows,
        lax.all_gather(pressure, "mode", axis=0, tiled=True),
        precision=lax.Precision.HIGHEST,
    )
    mixed_rim = padded(mixed.reshape(KL * local_modes, width, plane), (("space", 1),), 1)
    mixed_rim = mixed_rim.reshape(KL, local_modes, width + 2, plane)
    coupled = jnp.sum(apply_operator(spread_faces, mixed_rim, 1.0, depth), axis=0)
    residual = source - (image + coupled)
    diagonal = diagonal_of(mean_faces, 1.0)
    correction = damping * residual / diagonal
    correction = smooth(correction, residual, mean_faces, diagonal, 1.0, depth, fine_margin)
    rest = residual - apply_operator(mean_faces, fine_margin(correction), 1.0, depth)
    rows_one = rows // 2
    depth_one = depth // 2
    half = width // 2
    coarse_rest = restrict(rest, rows, depth)
    coarse_field = restrict(fields[0:1], rows, depth)
    place = lax.axis_index("space") * half
    whole_rest, whole_field = (
        lax.all_gather(coarse_rest, "space", axis=1, tiled=True),
        lax.all_gather(coarse_field, "space", axis=1, tiled=True),
    )
    whole_correction = cycle(whole_rest, whole_field, 1, rows_one, depth_one)
    lower = lax.dynamic_slice_in_dim(whole_correction, place, half, axis=1)
    correction = correction + prolong(lower, rows_one, depth_one)
    for turn in range(SWEEPS):
        correction = smooth(correction, residual, mean_faces, diagonal, 1.0, depth, fine_margin)
    shape = (local_modes, width, rows, depth)
    return (correction.reshape(shape), residual.reshape(shape))


def solution(mesh):
    in_specs = (
        P("mode", "space", None, None),
        P("mode", "space", None, None),
        P(None, "space", None, None),
        P(),
    )
    out_specs = (P("mode", "space", None, None), P("mode", "space", None, None))
    return jax.shard_map(local, mesh=mesh, in_specs=in_specs, out_specs=out_specs, check_vma=False)
```

profile of v0, /device:TPU:32, one launch (start us, length us, event | category | flops | bytes accessed | tf_op | source)
XLA Modules:
  0.0 704.8 jit_solution(4236844532845338030)
XLA Ops:
  37.4 131.6 %all-gather.3.cloned.1.call-done = f32[56,8,4096]{2,1,0:T(8,128)} async-done(((f32[7,8,4096]{2,1,0:T(8,128)}), f32[56,8,4096]{2,1,0:T(8,128)}) %all-gather.3.cloned.1.call-update) | async-done | bytes 7340048 | tf_op jit(solution)/shard_map/all_gather | solution.py:188
  169.0 13.9 %fusion = f32[5,7,8,4096]{3,1,2,0:T(8,128)S(1)} fusion(f32[56,8,4096]{2,1,0:T(8,128)} %all-gather.3.cloned.1.call-done, f32[56,5,56]{2,0,1:T(8,128)} %fusion.132, s32[]{:T(128)S(6)} %select_n.455), kind=kOutput, calls=%fused_computation.8 | convolution fusion | flops 770703360 | bytes 11948036 | tf_op jit(solution)/shard_map/kij,jxn->kixn/dot_general | solution.py:185
  211.7 10.1 %fusion.10 = f32[7,8,4096]{2,0,1:T(8,128)S(1)} fusion(f32[5,7,8,4096]{3,1,2,0:T(8,128)S(1)} %fusion, f32[5,7,1,4096]{3,1,2,0:T(8,128)S(1)} %copy.121, f32[5,7,1,4096]{3,1,2,0:T(8,128)S(1)} %copy.119, f32[5,7,8,4095]{3,1,2,0:T(8,128)} %get-tuple-element.76, f32[5,7,8,4095]{3,1,2,0:T(8,128)S(1)} %get-tuple-element.75, f32[5,7,8,3968]{3,1,2,0:T(8,128)} %get-tuple-element.74, ...), kind=kLoop, calls=%fused_computation.19 | loop fusion | flops 25001984 | bytes 28653376 | tf_op jit(solution)/shard_map/reduce_sum | solution.py:193
  228.9 5.8 collective-permute-done.5
  241.0 5.8 collective-permute-done.7
  250.6 16.2 %slice.1275 = f32[7,8,32,64]{3,2,0,1:T(8,128)} slice(f32[7,8,32,128]{3,2,0,1:T(8,128)S(1)} %reshape.140), slice={[0:7:1], [0:8:1], [0:32:1], [0:128:2]} | slice | bytes 917504 | tf_op jit(solution)/shard_map/slice | solution.py:92
  266.8 16.4 %slice.1276 = f32[7,8,32,64]{3,2,0,1:T(8,128)} slice(f32[7,8,32,128]{3,2,0,1:T(8,128)S(1)} %reshape.140), slice={[0:7:1], [0:8:1], [0:32:1], [1:128:2]} | slice | bytes 917504 | tf_op jit(solution)/shard_map/slice | solution.py:92
  297.6 32.8 %all_gather.11 = f32[1,128,1024]{2,0,1:T(1,128)S(1)} all-gather(f32[1,4,1024]{2,0,1:T(1,128)S(1)} %add_multiply_fusion.10), channel_id=1, replica_groups=mesh['space'=32,'mode'=8] {'space'}, dimensions={1}, use_global_device_ids=true | all-gather | bytes 540672 | tf_op jit(solution)/shard_map/all_gather | solution.py:207
  341.6 5.3 add_multiply_fusion
  426.8 5.3 copy.129
  437.5 5.7 fusion.24
  451.1 12.1 %slice.1305 = f32[7,128,16,32]{1,3,2,0:T(8,128)} slice(f32[7,128,16,64]{1,3,2,0:T(8,128)} %bitcast.213), slice={[0:7:1], [0:128:1], [0:16:1], [0:64:2]} | slice | bytes 3670016 | tf_op jit(solution)/shard_map/slice | solution.py:92
  463.2 12.1 %slice.1306 = f32[7,128,16,32]{1,3,2,0:T(8,128)} slice(f32[7,128,16,64]{1,3,2,0:T(8,128)} %bitcast.214), slice={[0:7:1], [0:128:1], [0:16:1], [1:64:2]} | slice | bytes 3670016 | tf_op jit(solution)/shard_map/slice | solution.py:92
  477.9 18.4 %slice.1309 = f32[7,64,256]{1,2,0:T(8,128)} slice(f32[7,128,256]{1,2,0:T(8,128)S(1)} %bitcast.249), slice={[0:7:1], [0:128:2], [0:256:1]} | slice | bytes 917504 | tf_op jit(solution)/shard_map/slice | solution.py:98
  496.4 18.7 %slice.1310 = f32[7,64,256]{1,2,0:T(8,128)} slice(f32[7,128,256]{1,2,0:T(8,128)S(1)} %bitcast.250), slice={[0:7:1], [1:128:2], [0:256:1]} | slice | bytes 917504 | tf_op jit(solution)/shard_map/slice | solution.py:98
  546.4 18.9 %subtract_divide_fusion.2 = (f32[1,7]{0,1:T(8,128)S(1)}, f32[1,7]{0,1:T(8,128)S(1)}, f32[1,7]{0,1:T(8,128)S(1)}, f32[1,7]{0,1:T(8,128)S(1)}, f32[1,7]{0,1:T(8,12...) fusion(f32[32,7]{0,1:T(8,128)S(1)} %bitcast.244, ...), kind=kLoop, calls=%fused_computation.302 | loop fusion | flops 616 | bytes 1496 | tf_op jit(solution)/shard_map/eval_jaxpr/div | solution.py:124
  565.2 11.6 %multiply_subtract_fusion.1 = (f32[1,7]{0,1:T(8,128)S(1)}, f32[1,7]{0,1:T(8,128)S(1)}, f32[1,7]{0,1:T(8,128)}, f32[1,7]{0,1:T(8,128)}, f32[1,7]{0,1:T(8,128)}, /...) fusion(f32[]{:T(128)S(6)} %div.1469, ...), kind=kLoop, calls=%fused_computation.269 | loop fusion | flops 777 | bytes 2048 | tf_op jit(solution)/shard_map/eval_jaxpr/sub | solution.py:124
  608.4 5.8 reshape_reshape.10
  618.9 5.5 reshape.131
  637.8 5.5 fusion.49
  647.6 5.9 fusion.57
  653.5 6.8 dynamic-slice_add_fusion
  676.7 5.9 collective-permute-done.9
  689.0 5.8 collective-permute-done.11
  (402 shorter events, 248.1 us)
Async XLA Ops:
  7.2 161.8 %all-gather.3.cloned.1.call-start = ((), (), s32[]{:S(2)}) async-start(), calls=%async_computation | async-start | bytes 8257536 | tf_op jit(solution)/shard_map/all_gather | solution.py:188
  9.6 417.2 %all-gather.5.cloned.1.call-start = ((), (), s32[]{:S(2)}) async-start(), calls=%async_computation.1 | async-start | bytes 4325376 | tf_op jit(solution)/shard_map/all_gather | solution.py:206
  12.0 23.6 %copy-start.3 = (f32[6,8,4096]{2,0,1:T(8,128)}, f32[6,8,4096]{2,0,1:T(8,128)S(1)}, u32[]{:S(2)}) copy-start(f32[6,8,4096]{2,0,1:T(8,128)S(1)} %copy.105) | copy-start | bytes 2359300
  12.9 13.5 %collective-permute-start = (f32[13,1,4096]{2,0,1:T(8,128)}, f32[13,1,4096]{2,0,1:T(8,128)S(1)}, u32[]{:S(2)}, u32[]{:S(2)}) collective-permute-start(f32[13,1,4096]{2,0,1:T(8,128)} %get-tuple-element.98), channel_id=1, source_target_pairs={{8,0},{16,8},{24,16},{32,24},{40,32},{48,40},{56,48},{64,56},{72,6... | collective-permute-start | bytes 638984 | tf_op jit(solution)/shard_map/ppermute | solution.py:26
  16.6 9.8 %collective-permute-start.1 = (f32[13,1,4096]{2,0,1:T(8,128)S(1)}, f32[13,1,4096]{2,0,1:T(8,128)S(1)}, u32[]{:S(2)}, u32[]{:S(2)}) collective-permute-start(f32[13,1,4096]{2,0,1:T(8,128)S(1)} %get-tuple-element.97), channel_id=1, source_target_pairs={{0,8},{8,16},{16,24},{24,32},{32,40},{40,48},{48,56},{56,64},{64,7... | collective-permute-start | bytes 638984 | tf_op jit(solution)/shard_map/ppermute | solution.py:24
  36.8 210.0 %copy-start.25 = (f32[1,8,4096]{2,1,0:T(8,128)}, f32[1,8,4096]{2,1,0:T(8,128)S(1)}, u32[]{:S(2)}) copy-start(f32[1,8,4096]{2,1,0:T(8,128)S(1)} %copy.190) | copy-start | bytes 393220
  37.0 209.8 %copy-start.27 = (f32[8,4096]{1,0:T(8,128)}, f32[8,4096]{1,0:T(8,128)S(1)}, u32[]{:S(2)}) copy-start(f32[8,4096]{1,0:T(8,128)S(1)} %get-tuple-element.328) | copy-start | bytes 393220
  37.0 209.8 %copy-start.29 = (f32[8,4096]{1,0:T(8,128)}, f32[8,4096]{1,0:T(8,128)S(1)}, u32[]{:S(2)}) copy-start(f32[8,4096]{1,0:T(8,128)S(1)} %get-tuple-element.329) | copy-start | bytes 393220
  37.2 209.6 %copy-start.31 = (f32[8,4096]{1,0:T(8,128)}, f32[8,4096]{1,0:T(8,128)S(1)}, u32[]{:S(2)}) copy-start(f32[8,4096]{1,0:T(8,128)S(1)} %get-tuple-element.330) | copy-start | bytes 393220
  37.2 209.6 %copy-start.33 = (f32[8,4096]{1,0:T(8,128)}, f32[8,4096]{1,0:T(8,128)S(1)}, u32[]{:S(2)}) copy-start(f32[8,4096]{1,0:T(8,128)S(1)} %get-tuple-element.331) | copy-start | bytes 393220
  37.4 197.3 %copy-start.42 = (f32[8,4096]{1,0:T(8,128)}, f32[8,4096]{1,0:T(8,128)S(1)}, u32[]{:S(2)}) copy-start(f32[8,4096]{1,0:T(8,128)S(1)} %get-tuple-element.326) | copy-start | bytes 393220
  37.4 209.5 %copy-start.35 = (f32[8,4096]{1,0:T(8,128)}, f32[8,4096]{1,0:T(8,128)S(1)}, u32[]{:S(2)}) copy-start(f32[8,4096]{1,0:T(8,128)S(1)} %get-tuple-element.327) | copy-start | bytes 393220
  191.7 12.5 %collective-permute-start.2 = (f32[35,1,4096]{2,1,0:T(1,128)}, f32[35,1,4096]{2,1,0:T(1,128)}, u32[]{:S(2)}, u32[]{:S(2)}) collective-permute-start(f32[35,1,4096]{2,1,0:T(1,128)} %get-tuple-element.77), channel_id=1, source_target_pairs={{8,0},{16,8},{24,16},{32,24},{40,32},{48,40},{56,48},{64,56},{72,6... | collective-permute-start | bytes 1720328 | tf_op jit(solution)/shard_map/ppermute | solution.py:26
  196.8 14.8 %copy-start.65 = (f32[5,8,4096]{2,1,0:T(8,128)S(1)}, f32[5,8,4096]{2,1,0:T(8,128)}, u32[]{:S(2)}) copy-start(f32[5,8,4096]{2,1,0:T(8,128)} %copy.116) | copy-start | bytes 1966084
  196.8 13.4 %collective-permute-start.3 = (f32[35,1,4096]{2,1,0:T(1,128)S(1)}, f32[35,1,4096]{2,1,0:T(1,128)}, u32[]{:S(2)}, u32[]{:S(2)}) collective-permute-start(f32[35,1,4096]{2,1,0:T(1,128)S(1)} %get-tuple-element.78), channel_id=1, source_target_pairs={{0,8},{8,16},{16,24},{24,32},{32,40},{40,48},{48,56},{56,64},{64,7... | collective-permute-start | bytes 1720328 | tf_op jit(solution)/shard_map/ppermute | solution.py:24
  224.4 4.5 collective-permute-start.4
  226.3 8.4 %collective-permute-start.5 = (f32[7,1,4096]{2,0,1:T(8,128)S(1)}, f32[7,1,4096]{2,0,1:T(8,128)S(1)}, u32[]{:S(2)}, u32[]{:S(2)}) collective-permute-start(f32[7,1,4096]{2,0,1:T(8,128)S(1)} %get-tuple-element.132), channel_id=1, source_target_pairs={{0,8},{8,16},{16,24},{24,32},{32,40},{40,48},{48,56},{56,64},{64,7... | collective-permute-start | bytes 344072 | tf_op jit(solution)/shard_map/ppermute | solution.py:24
  236.5 4.5 collective-permute-start.6
  238.4 8.4 %collective-permute-start.7 = (f32[7,1,4096]{2,0,1:T(8,128)S(1)}, f32[7,1,4096]{2,0,1:T(8,128)S(1)}, u32[]{:S(2)}, u32[]{:S(2)}) collective-permute-start(f32[7,1,4096]{2,0,1:T(8,128)S(1)} %get-tuple-element.126), channel_id=1, source_target_pairs={{0,8},{8,16},{16,24},{24,32},{32,40},{40,48},{48,56},{56,64},{64,7... | collective-permute-start | bytes 344072 | tf_op jit(solution)/shard_map/ppermute | solution.py:24
  348.2 83.9 %copy-start.22 = (f32[1,128,1024]{1,2,0:T(8,128)}, f32[1,128,1024]{1,2,0:T(8,128)S(1)}, u32[]{:S(2)}) copy-start(f32[1,128,1024]{1,2,0:T(8,128)S(1)} %copy.155) | copy-start | bytes 1572868
  670.5 6.2 collective-permute-start.8
  674.2 8.4 %collective-permute-start.9 = (f32[7,1,4096]{2,0,1:T(8,128)S(1)}, f32[7,1,4096]{2,0,1:T(8,128)S(1)}, u32[]{:S(2)}, u32[]{:S(2)}) collective-permute-start(f32[7,1,4096]{2,0,1:T(8,128)S(1)} %get-tuple-element.120), channel_id=1, source_target_pairs={{0,8},{8,16},{16,24},{24,32},{32,40},{40,48},{48,56},{56,64},{64,7... | collective-permute-start | bytes 344072 | tf_op jit(solution)/shard_map/ppermute | solution.py:24
  684.5 4.5 collective-permute-start.10
  686.4 8.4 %collective-permute-start.11 = (f32[7,1,4096]{2,0,1:T(8,128)S(1)}, f32[7,1,4096]{2,0,1:T(8,128)S(1)}, u32[]{:S(2)}, u32[]{:S(2)}) collective-permute-start(f32[7,1,4096]{2,0,1:T(8,128)S(1)} %get-tuple-element.114), channel_id=1, source_target_pairs={{0,8},{8,16},{16,24},{24,32},{32,40},{40,48},{48,56},{56,64},{64,7... | collective-permute-start | bytes 344072 | tf_op jit(solution)/shard_map/ppermute | solution.py:24
  (76 other events, 346.8 us)
Sparse Core Ops, SparseCore 0:
  11.2 157.7 all-gather.2
  292.8 56.4 all-gather.4
where the time goes:
time: 716 us; the launch traced here: 705 us
  local copies, waits for them, and re-layouts  274 us (38%)
  waiting for transfers between devices  160 us (22%)
  other arithmetic  117 us (16%)
  between operations  74.9 us (10%)
  blocking collectives  32.8 us (5%)
  starting transfers between devices  31.7 us (4%)
  matrix products  14.8 us (2%)
    all_gather x1, waiting for transfers between devices, local(): lax.all_gather(pressure, 'mode', axis=0, tiled=True)  132 us
    slice x12, local copies, waits for them, and re-layouts, pair_yz(): cells = cells[..., 0::2] + cells[..., 1::2]  72.5 us
    slice x10, local copies, waits for them, and re-layouts, pair_x(): return values[..., 0::2, :] + values[..., 1::2, :]  50.9 us
    all_gather x1, blocking collectives, local(): lax.all_gather(coarse_field, 'space', axis=1, tiled=True)  32.8 us
    add x16, other arithmetic, smooth(): correction + damping * (residual - apply_operator(faces, margin(correctio...  28.6 us
    ppermute x6, waiting for transfers between devices, padded(): lax.ppermute(tail, axis, [(i, (i + 1) % count) for i in range(ends)])  27.9 us
    slice x46, local copies, waits for them, and re-layouts, along_last(): return jnp.concatenate([values[..., offset:], zeros], axis=-1)  25.7 us
    div x1, other arithmetic, line_solve(): solved = lax.linalg.tridiagonal_solve(below, middle, above, right)  18.9 us
  transfers between devices with their start and end apart: 14, of which 8 were waited for; matrix products, arithmetic and copies ran while one was open for 10% of the time, Pallas kernels for 0%

commit v1 on v0

v1 whole, which is shorter than its diff:
```python
import jax
import jax.numpy as jnp
from jax import lax
from jax.sharding import PartitionSpec as P
from jax.experimental import pallas as pl
from jax.experimental.pallas import tpu as pltpu

MESH = pl.DeviceIdType.MESH
F32 = jnp.float32
P_SIZE = 56
KL = 5
SWEEPS = 2
COARSE = 8
LEVELS = 4
LANES = 128
ROW = 8
COLS = 4
PAD = 16


def split_dot(values, matrix):
    high = values.astype(jnp.bfloat16)
    low = (values - high.astype(F32)).astype(jnp.bfloat16)
    return jnp.dot(high, matrix, preferred_element_type=F32) + jnp.dot(
        low, matrix, preferred_element_type=F32
    )


def pairing():
    wide = lax.broadcasted_iota(jnp.int32, (2 * LANES, LANES), 0)
    narrow = lax.broadcasted_iota(jnp.int32, (2 * LANES, LANES), 1)
    return jnp.where(wide // 2 == narrow, 1.0, 0.0).astype(jnp.bfloat16)


def spreading():
    narrow = lax.broadcasted_iota(jnp.int32, (LANES, 2 * LANES), 0)
    wide = lax.broadcasted_iota(jnp.int32, (LANES, 2 * LANES), 1)
    return jnp.where(wide // 2 == narrow, 1.0, 0.0).astype(jnp.bfloat16)


def level_faces(coef, faces, weight, inverse, first, count, step, rows, depth, scale, origin, width):
    bits = rows.bit_length() - 1
    lane = lax.broadcasted_iota(jnp.int32, (step, LANES), 1) & (depth - 1)
    place = lax.broadcasted_iota(jnp.int32, (step, LANES), 0)

    @pl.loop(0, count // step)
    def _(turn):
        base = pl.multiple_of(first + turn * step, 8)
        at = place + (base - PAD)
        y = at & (rows - 1)
        x = (at >> bits) + origin
        inside = jnp.logical_and(x >= 0, x < width)
        c = coef[pl.ds(base, step), :]
        others = (
            (coef[pl.ds(base + rows, step), :], None),
            (coef[pl.ds(base - rows, step), :], None),
            (coef[pl.ds(base + 1, step), :], y < rows - 1),
            (coef[pl.ds(base - 1, step), :], y > 0),
            (pltpu.roll(c, LANES - 1, 1), lane < depth - 1),
            (pltpu.roll(c, 1, 1), lane > 0),
        )
        sides = []
        total = jnp.zeros_like(c)
        for other, keep in others:
            face = 0.5 * (c + other)
            if keep is not None:
                face = jnp.where(keep, face, 0.0)
            sides.append(face)
            total = total + face
        part = jnp.where(inside, 0.8 / jnp.where(inside, total, 1.0), 0.0)
        weight[pl.ds(base, step), :] = part * (1.0 / scale)
        inverse[pl.ds(base, step), :] = jnp.where(inside, total * (scale * 1.25), 0.0)
        for n in range(6):
            faces[n, pl.ds(base, step), :] = part * sides[n]


def first_sweep(start, right, weight, modes, first, count, step):
    @pl.loop(0, count // step)
    def _(turn):
        base = pl.multiple_of(first + turn * step, 8)
        w = weight[pl.ds(base, step), :]
        for m in range(modes):
            start[m, pl.ds(base, step), :] = w * right[m, pl.ds(base, step), :]


def sweep(out, now, start, faces, modes, first, count, step, rows, keep=0.2, inverse=None):
    @pl.loop(0, count // step)
    def _(turn):
        base = pl.multiple_of(first + turn * step, 8)
        g = [faces[n, pl.ds(base, step), :] for n in range(6)]
        for m in range(modes):
            c = now[m, pl.ds(base, step), :]
            total = start[m, pl.ds(base, step), :] + (keep if inverse is None else -0.8) * c
            total = total + g[0] * now[m, pl.ds(base + rows, step), :]
            total = total + g[1] * now[m, pl.ds(base - rows, step), :]
            total = total + g[2] * now[m, pl.ds(base + 1, step), :]
            total = total + g[3] * now[m, pl.ds(base - 1, step), :]
            total = total + g[4] * pltpu.roll(c, LANES - 1, 1)
            total = total + g[5] * pltpu.roll(c, 1, 1)
            if inverse is not None:
                total = total * inverse[pl.ds(base, step), :]
            out[m, pl.ds(base, step), :] = total


def pair_xy(values, first, planes, rows, temp):
    for x in range(planes // 2):
        temp[pl.ds(x * rows, rows), :] = (
            values[pl.ds(first + 2 * x * rows, rows), :]
            + values[pl.ds(first + (2 * x + 1) * rows, rows), :]
        )
    half = planes // 2 * rows // 2
    return temp[pl.ds(0, half, 2), :] + temp[pl.ds(1, half, 2), :]


def restrict_pair(left, right, matrix):
    return 0.125 * split_dot(jnp.concatenate([left, right], axis=-1), matrix)


def prolong(fine, modes, fine_first, coarse, coarse_first, planes, rows, matrix, temp):
    count = planes * rows
    for p in range((modes + 1) // 2):
        both = split_dot(coarse[p, pl.ds(coarse_first, count), :], matrix)
        for part in range(2):
            m = 2 * p + part
            if m >= modes:
                continue
            child = both[:, part * LANES : (part + 1) * LANES]
            temp[pl.ds(0, count, 2), :] = child
            temp[pl.ds(1, count, 2), :] = child
            for x in range(planes):
                child_plane = temp[pl.ds(2 * x * rows, 2 * rows), :]
                for side in range(2):
                    at = pl.ds(fine_first + (2 * x + side) * 2 * rows, 2 * rows)
                    fine[m, at, :] = fine[m, at, :] + child_plane


def zero_all(ref):
    ref[...] = jnp.zeros(ref.shape, ref.dtype)


def cycle_kernel(
    geometry, b_ref, field_ref, out_ref,
    c0, w0, i0, g0, b0, s0, a0, d0,
    c1, w1, i1, g1, b1, s1, a1, d1,
    c2, w2, i2, g2, b2, s2, a2, d2,
    c3, w3, i3, g3, b3, s3, a3, d3,
    temp, line, sums, send_sem, recv_sem,
):
    modes, width, rows, blocks = geometry
    grid = width * blocks
    me = lax.axis_index("space")
    mode = lax.axis_index("mode")
    r1, r2, r3 = rows // 2, rows // 4, rows // 8
    n1, n2 = width // 2, width // 4
    row_at, col_at = me % ROW, me // ROW
    cols = blocks // ROW
    counter = [0]

    def start_copy(src, dst, target, exists=None):
        number = counter[0]
        counter[0] += 1
        copy = pltpu.make_async_remote_copy(
            src_ref=src, dst_ref=dst, send_sem=send_sem.at[number], recv_sem=recv_sem.at[number],
            device_id=(target, mode), device_id_type=MESH,
        )
        if exists is None:
            copy.start()
        else:
            pl.when(exists)(copy.start)
        return copy

    def shift_exists(delta):
        return me + delta < blocks if delta > 0 else me + delta >= 0

    sends = []

    def to_neighbour(src, dst, delta):
        copy = start_copy(src, dst, me + delta, shift_exists(delta))
        sends.append((copy, shift_exists(delta)))
        return (copy, shift_exists(-delta))

    def arrived(pair):
        copy, exists = pair
        if exists is None:
            copy.wait_recv()
        else:
            pl.when(exists)(copy.wait_recv)

    def row_peer(q):
        return col_at * ROW + (row_at + q) % ROW

    def col_peer(q):
        return ((col_at + q) % cols) * ROW + row_at

    for ref in (c0, b0, s0, a0, d0, c1, b1, s1, a1, d1, c2, b2, s2, a2, d2, c3, b3, s3, a3, d3):
        zero_all(ref)

    barrier = pltpu.get_barrier_semaphore()
    expected = ROW - 1 + cols - 1
    for delta in (1, -1, 2, -2):
        @pl.when(shift_exists(delta))
        def _():
            pl.semaphore_signal(barrier, inc=1, device_id=(me + delta, mode), device_id_type=MESH)
        expected = expected + jnp.where(shift_exists(delta), 1, 0)
    for q in range(1, ROW):
        pl.semaphore_signal(barrier, inc=1, device_id=(row_peer(q), mode), device_id_type=MESH)
    for q in range(1, cols):
        pl.semaphore_signal(barrier, inc=1, device_id=(col_peer(q), mode), device_id_type=MESH)
    pl.semaphore_wait(barrier, expected)

    own0 = PAD + 4 * rows
    size0 = width * rows
    halos = []
    halos.append(to_neighbour(b_ref.at[:, pl.ds(size0 - 3 * rows, 3 * rows)], b0.at[pl.ds(0, modes), pl.ds(own0 - 3 * rows, 3 * rows)], 1))
    halos.append(to_neighbour(b_ref.at[:, pl.ds(0, 3 * rows)], b0.at[pl.ds(0, modes), pl.ds(own0 + size0, 3 * rows)], -1))
    c_halos = []
    c_halos.append(to_neighbour(field_ref.at[0, pl.ds(size0 - 4 * rows, 4 * rows)], c0.at[pl.ds(own0 - 4 * rows, 4 * rows)], 1))
    c_halos.append(to_neighbour(field_ref.at[0, pl.ds(0, 4 * rows)], c0.at[pl.ds(own0 + size0, 4 * rows)], -1))
    c0[pl.ds(own0, size0), :] = field_ref[0]
    for m in range(modes):
        b0[m, pl.ds(own0, size0), :] = b_ref[m]

    merge = pairing()
    spread = spreading()

    own1 = PAD + 5 * r1
    size1 = n1 * r1
    part = pair_xy(c0, own0, width, rows, temp)
    c1[pl.ds(own1, size1), :] = restrict_pair(part, part, merge)
    c1_halos = [
        to_neighbour(c1.at[pl.ds(own1, size1)], c1.at[pl.ds(own1 - size1, size1)], 1),
        to_neighbour(c1.at[pl.ds(own1, size1)], c1.at[pl.ds(own1 + size1, size1)], -1),
        to_neighbour(c1.at[pl.ds(own1 + size1 - r1, r1)], c1.at[pl.ds(own1 - size1 - r1, r1)], 2),
        to_neighbour(c1.at[pl.ds(own1, r1)], c1.at[pl.ds(own1 + 2 * size1, r1)], -2),
    ]
    size2 = n2 * r2
    own2 = pl.multiple_of(PAD + me * size2, 8)
    group2 = pl.multiple_of(PAD + col_at * (ROW * size2), 8)
    part = pair_xy(c1, own1, n1, r1, temp)
    c2[pl.ds(own2, size2), :] = restrict_pair(part, part, merge)
    c2_row = []
    for q in range(1, ROW):
        copy = start_copy(c2.at[pl.ds(own2, size2)], c2.at[pl.ds(own2, size2)], row_peer(q))
        sends.append((copy, None))
        c2_row.append((copy, None))

    for pair in c_halos:
        arrived(pair)
    level_faces(c0, g0, w0, i0, PAD + rows, (width + 6) * rows, 16, rows, LANES, 1.0, me * width - 4, grid)

    for pair in c2_row:
        arrived(pair)
    c2_col = []
    for q in range(1, cols):
        at = pl.ds(group2, ROW * size2)
        copy = start_copy(c2.at[at], c2.at[at], col_peer(q))
        sends.append((copy, None))
        c2_col.append((copy, None))
    for pair in c1_halos:
        arrived(pair)
    level_faces(c1, g1, w1, i1, PAD + r1, (n1 + 8) * r1, 16, r1, LANES // 2, 0.25, me * n1 - 5, grid // 2)
    for pair in c2_col:
        arrived(pair)
    all2 = blocks * size2
    level_faces(c2, g2, w2, i2, PAD, all2, 32, r2, LANES // 4, 0.0625, 0, grid // 4)
    part = pair_xy(c2, PAD, blocks * n2, r2, temp)
    all3 = all2 // 4
    c3[pl.ds(PAD, all3), :] = restrict_pair(part, part, merge)
    level_faces(c3, g3, w3, i3, PAD, all3, 32, r3, LANES // 8, 0.015625, 0, grid // 8)
    columns = grid // 8
    gather = jnp.where(
        lax.broadcasted_iota(jnp.int32, (columns, all3), 1) // r3
        == lax.broadcasted_iota(jnp.int32, (columns, all3), 0), 1.0, 0.0)
    within = jnp.where(
        lax.broadcasted_iota(jnp.int32, (LANES, LANES), 1) // (LANES // 8)
        == lax.broadcasted_iota(jnp.int32, (LANES, LANES), 0) // (LANES // 8), 1.0, 0.0)

    def column_sums(values):
        return jnp.dot(
            jnp.dot(gather, values, precision=lax.Precision.HIGHEST, preferred_element_type=F32),
            within, precision=lax.Precision.HIGHEST, preferred_element_type=F32)

    diag3 = i3[pl.ds(PAD, all3), :]
    line[0] = column_sums(g3[1, pl.ds(PAD, all3), :] * diag3)
    line[2] = column_sums(g3[0, pl.ds(PAD, all3), :] * diag3)
    ratio = None
    for x in range(columns):
        low, high = line[0, pl.ds(x, 1), :], line[2, pl.ds(x, 1), :]
        den = low + high
        if ratio is not None:
            den = den - low * ratio
        inv = 1.0 / den
        ratio = high * inv
        line[0, pl.ds(x, 1), :] = low * inv
        line[1, pl.ds(x, 1), :] = inv
        line[2, pl.ds(x, 1), :] = ratio

    for pair in halos:
        arrived(pair)
    first_sweep(s0, b0, w0, modes, PAD + rows, (width + 6) * rows, 16)
    sweep(a0, s0, s0, g0, modes, PAD + 2 * rows, (width + 4) * rows, 16, rows)
    sweep(d0, a0, s0, g0, modes, own0, size0, 16, rows, inverse=i0)

    pairs1 = b1.shape[0]
    for p in range(pairs1):
        left = pair_xy(d0.at[2 * p], own0, width, rows, temp)
        right = pair_xy(d0.at[2 * p + 1], own0, width, rows, temp)
        b1[p, pl.ds(own1, size1), :] = restrict_pair(left, right, merge)
    b1_halos = [
        to_neighbour(b1.at[:, pl.ds(own1, size1)], b1.at[:, pl.ds(own1 - size1, size1)], 1),
        to_neighbour(b1.at[:, pl.ds(own1, size1)], b1.at[:, pl.ds(own1 + size1, size1)], -1),
    ]
    for pair in b1_halos:
        arrived(pair)
    first_sweep(s1, b1, w1, pairs1, PAD + r1, (n1 + 8) * r1, 16)
    sweep(a1, s1, s1, g1, pairs1, PAD + 2 * r1, (n1 + 6) * r1, 16, r1)
    sweep(d1, a1, s1, g1, pairs1, own1, size1, 16, r1, inverse=i1)
    pairs2 = b2.shape[0]
    for p in range(pairs2):
        left = pair_xy(d1.at[2 * p], own1, n1, r1, temp)
        right = pair_xy(d1.at[2 * p + 1], own1, n1, r1, temp)
        b2[p, pl.ds(own2, size2), :] = restrict_pair(left, right, merge)
    row_copies = []
    for q in range(1, ROW):
        at = pl.ds(own2, size2)
        copy = start_copy(b2.at[:, at], b2.at[:, at], row_peer(q))
        sends.append((copy, None))
        row_copies.append((copy, None))
    for pair in row_copies:
        arrived(pair)
    col_copies = []
    for q in range(1, cols):
        at = pl.ds(group2, ROW * size2)
        copy = start_copy(b2.at[:, at], b2.at[:, at], col_peer(q))
        sends.append((copy, None))
        col_copies.append((copy, None))
    for pair in col_copies:
        arrived(pair)

    first_sweep(s2, b2, w2, pairs2, PAD, all2, 32)
    sweep(a2, s2, s2, g2, pairs2, PAD, all2, 32, r2)
    sweep(d2, a2, s2, g2, pairs2, PAD, all2, 32, r2, inverse=i2)
    left = pair_xy(d2.at[0], PAD, blocks * n2, r2, temp)
    right = pair_xy(d2.at[1], PAD, blocks * n2, r2, temp)
    b3[0, pl.ds(PAD, all3), :] = restrict_pair(left, right, merge)
    first_sweep(s3, b3, w3, 1, PAD, all3, 32)
    now, other = s3, a3
    for turn in range(COARSE - 1):
        sweep(other, now, s3, g3, 1, PAD, all3, 32, r3)
        now, other = (a3, d3) if now is s3 else (other, now)
    sweep(b3, now, s3, g3, 1, PAD, all3, 32, r3, inverse=i3)
    sums[...] = column_sums(b3[0, pl.ds(PAD, all3), :])
    carried = None
    for x in range(columns):
        value = sums[pl.ds(x, 1), :] * line[1, pl.ds(x, 1), :]
        if carried is not None:
            value = value + line[0, pl.ds(x, 1), :] * carried
        sums[pl.ds(x, 1), :] = value
        carried = value
    carried = None
    for x in reversed(range(columns)):
        value = sums[pl.ds(x, 1), :]
        if carried is not None:
            value = value + line[2, pl.ds(x, 1), :] * carried
        carried = value
        at = pl.ds(PAD + x * r3, r3)
        now[0, at, :] = now[0, at, :] + jnp.broadcast_to(value, (r3, LANES))
    prolong(a2, pairs2, PAD, now, PAD, columns, r3, spread, temp)
    sweep(d2, a2, s2, g2, pairs2, PAD, all2, 32, r2)
    sweep(a2, d2, s2, g2, pairs2, PAD, all2, 32, r2)
    window = pl.multiple_of(PAD + me * size2 - 2 * r2, 8)
    prolong(a1, pairs1, PAD + r1, a2, window, n2 + 4, r2, spread, temp)
    sweep(d1, a1, s1, g1, pairs1, PAD + 3 * r1, (n1 + 4) * r1, 16, r1)
    sweep(a1, d1, s1, g1, pairs1, PAD + 4 * r1, (n1 + 2) * r1, 16, r1)
    prolong(a0, modes, PAD + 2 * rows, a1, PAD + 4 * r1, n1 + 2, r1, spread, temp)
    sweep(d0, a0, s0, g0, modes, PAD + 3 * rows, (width + 2) * rows, 16, rows)
    sweep(a0, d0, s0, g0, modes, own0, size0, 16, rows)
    for m in range(modes):
        out_ref[m] = a0[m, pl.ds(own0, size0), :]
    for copy, exists in sends:
        if exists is None:
            copy.wait_send()
        else:
            pl.when(exists)(copy.wait_send)


def vcycle(residual, fields, blocks):
    modes, width, rows, depth = residual.shape
    plane = width * rows
    even = modes + modes % 2
    r1, r2, r3 = rows // 2, rows // 4, rows // 8
    grid = width * blocks
    n0 = (width + 8) * rows + 2 * PAD
    n1 = (width // 2 + 10) * r1 + 2 * PAD
    n2 = grid // 4 * r2 + 2 * PAD
    n3 = grid // 8 * r3 + 2 * PAD
    scratch = []
    for size, count in ((n0, even), (n1, even // 2), (n2, even // 4), (n3, 1)):
        scratch += [pltpu.VMEM((size, LANES), F32)] * 3
        scratch += [pltpu.VMEM((6, size, LANES), F32)]
        scratch += [pltpu.VMEM((count, size, LANES), F32)] * 4
    copies = 4 + 4 + 2 + 2 * (ROW - 1 + blocks // ROW - 1)
    scratch += [
        pltpu.VMEM((grid // 4 * r2, LANES), F32),
        pltpu.VMEM((3, grid // 8, LANES), F32),
        pltpu.VMEM((grid // 8, LANES), F32),
        pltpu.SemaphoreType.DMA((copies,)),
        pltpu.SemaphoreType.DMA((copies,)),
    ]
    geometry = (modes, width, rows, blocks)
    out = pl.pallas_call(
        lambda *refs: cycle_kernel(geometry, *refs),
        out_shape=jax.ShapeDtypeStruct((modes, plane, depth), F32),
        in_specs=[pl.BlockSpec(memory_space=pltpu.VMEM)] * 2,
        out_specs=pl.BlockSpec(memory_space=pltpu.VMEM),
        scratch_shapes=scratch,
        compiler_params=pltpu.CompilerParams(
            collective_id=1, has_side_effects=True, vmem_limit_bytes=56 * 2**20),
        name="vcycle",
    )(residual.reshape(modes, plane, depth), fields[0:1].reshape(1, plane, depth))
    return out.reshape(residual.shape)


def padded(cells, sides, width):
    for axis, dim in sides:
        count = lax.axis_size(axis)
        ends = count - 1
        head = lax.slice_in_dim(cells, 0, width, axis=dim)
        tail = lax.slice_in_dim(cells, cells.shape[dim] - width, cells.shape[dim], axis=dim)
        cells = jnp.concatenate(
            [
                lax.ppermute(tail, axis, [(i, (i + 1) % count) for i in range(ends)]),
                cells,
                lax.ppermute(head, axis, [((i + 1) % count, i) for i in range(ends)]),
            ],
            axis=dim,
        )
    return cells


def along_last(values, offset):
    size = values.shape[-1]
    zeros = jnp.zeros(values.shape[:-1] + (abs(offset),), values.dtype)
    if offset > 0:
        return jnp.concatenate([values[..., offset:], zeros], axis=-1)
    return jnp.concatenate([zeros, values[..., : size + offset]], axis=-1)


def neighbours(values_rim, depth):
    values = values_rim[..., 1:-1, :]
    positions = lax.iota(jnp.int32, values.shape[-1]) % depth
    upper = positions < depth - 1
    lower = positions > 0
    others = (
        values_rim[..., 2:, :],
        values_rim[..., :-2, :],
        along_last(values, depth),
        along_last(values, -depth),
        jnp.where(upper, along_last(values, 1), 0.0),
        jnp.where(lower, along_last(values, -1), 0.0),
    )
    return (values, others)


def faces_of(field_rim, depth):
    field, others = neighbours(field_rim, depth)
    plane = field.shape[-1]
    places = lax.iota(jnp.int32, plane)
    within = places % depth
    inside = (places < plane - depth, places >= depth, within < depth - 1, within > 0)
    collected = [0.5 * (field + others[0]), 0.5 * (field + others[1])]
    for keep, other in zip(inside, others[2:]):
        collected.append(jnp.where(keep, 0.5 * (field + other), 0.0))
    return collected


def apply_operator(faces, values_rim, scale, depth):
    values, others = neighbours(values_rim, depth)
    total = faces[0] * (values - others[0])
    for face, other in zip(faces[1:], others[1:]):
        total = total + face * (values - other)
    return scale * total


def diagonal_of(faces, scale):
    total = faces[0]
    for face in faces[1:]:
        total = total + face
    return scale * total


def coupling_tables(coupling_list):
    modes = jnp.arange(P_SIZE, dtype=jnp.int32)
    orders = jnp.arange(1, KL + 1, dtype=jnp.int32)
    firsts = (coupling_list[0][:, None] == modes[None, :]).astype(jnp.float32)
    seconds = (coupling_list[1][:, None] == modes[None, :]).astype(jnp.float32)
    weights = jnp.sqrt(coupling_list[3].astype(jnp.float32))
    which = (coupling_list[2][:, None] == orders[None, :]).astype(jnp.float32) * weights[:, None]
    return jnp.einsum("nk,ni,nj->kij", which, firsts, seconds, precision=lax.Precision.HIGHEST)


def local(blocks, pressure, source, kl_field, coupling_list):
    local_modes, width, rows, depth = pressure.shape
    plane = rows * depth
    pressure = pressure.reshape(local_modes, width, plane)
    source = source.reshape(local_modes, width, plane)
    fields = kl_field.reshape(kl_field.shape[0], width, plane)
    joined = padded(jnp.concatenate([pressure, fields], axis=0), (("space", 1),), 1)
    pressure_rim = joined[:local_modes]
    field_rim = joined[local_modes:]
    mean_faces = faces_of(field_rim[0:1], depth)
    spread_faces = faces_of(field_rim[1:, None], depth)
    image = apply_operator(mean_faces, pressure_rim, 1.0, depth)
    tables = coupling_tables(coupling_list)
    first = lax.axis_index("mode") * local_modes
    own_rows = lax.dynamic_slice_in_dim(tables, first, local_modes, axis=1)
    mixed = jnp.einsum(
        "kij,jxn->kixn",
        own_rows,
        lax.all_gather(pressure, "mode", axis=0, tiled=True),
        precision=lax.Precision.HIGHEST,
    )
    mixed_rim = padded(mixed.reshape(KL * local_modes, width, plane), (("space", 1),), 1)
    mixed_rim = mixed_rim.reshape(KL, local_modes, width + 2, plane)
    coupled = jnp.sum(apply_operator(spread_faces, mixed_rim, 1.0, depth), axis=0)
    residual = source - (image + coupled)
    shape = (local_modes, width, rows, depth)
    residual = residual.reshape(shape)
    return (vcycle(residual, kl_field, blocks), residual)


def solution(mesh):
    in_specs = (
        P("mode", "space", None, None),
        P("mode", "space", None, None),
        P(None, "space", None, None),
        P(),
    )
    out_specs = (P("mode", "space", None, None), P("mode", "space", None, None))
    blocks = mesh.shape["space"]
    return jax.shard_map(lambda *arrays: local(blocks, *arrays), mesh=mesh, in_specs=in_specs, out_specs=out_specs, check_vma=False)
```

time: 716 us -> 302 us (0.42); the launches traced: 705 us -> 301 us
  local copies, waits for them, and re-layouts: 274 us -> 44 us
  other arithmetic: 117 us -> 14.4 us
  Pallas kernels: 0 us -> 65.5 us
  between operations: 74.9 us -> 14.5 us
  blocking collectives: 32.8 us -> 0 us
  waiting for transfers between devices: 160 us -> 135 us
  starting transfers between devices: 31.7 us -> 12.9 us
    slice x40 -> x0, local copies, waits for them, and re-layouts: 136 us -> none  [the longest x12 72.5 us: pair_yz(): cells = cells[..., 0::2] + cells[..., 1::2]]
    pallas_call x0 -> x1, Pallas kernels: none -> 65.5 us  [vcycle(): pl.pallas_call(lambda *refs: cycle_kernel(geometry, *refs), out_shape=jax...]
    add x34 -> x0, other arithmetic: 50 us -> none  [the longest x16 28.6 us: smooth(): correction + damping * (residual - apply_operator(faces, margin(correctio...]
    all_gather x1 -> x0, blocking collectives: 32.8 us -> none  [local(): lax.all_gather(coarse_field, 'space', axis=1, tiled=True)]
    reshape x16 -> x2, local copies, waits for them, and re-layouts: 32 us -> 1.48 us  [local(): residual = residual.reshape(shape)]
    div x5 -> x0, other arithmetic: 26.2 us -> none  [the longest x1 18.9 us: line_solve(): solved = lax.linalg.tridiagonal_solve(below, middle, above, right)]
    ppermute x6 -> x2, waiting for transfers between devices: 27.9 us -> 4.49 us  [padded(): lax.ppermute(tail, axis, [(i, (i + 1) % count) for i in range(ends)])]
    sub x4 -> x1, other arithmetic: 20.4 us -> 2.07 us  [local(): residual = source - (image + coupled)]
  transfers between devices with their start and end apart: 14 -> 5, of which waited for: 8 -> 3; matrix products, arithmetic and copies ran while one was open for 10% -> 10% of each run, Pallas kernels for 0% -> 0%
where the time goes in v1:
time: 302 us; the launch traced here: 301 us
  waiting for transfers between devices  135 us (45%)
  Pallas kernels  65.5 us (22%)
  local copies, waits for them, and re-layouts  44 us (15%)
  matrix products  14.7 us (5%)
  between operations  14.5 us (5%)
  other arithmetic  14.4 us (5%)
  starting transfers between devices  12.9 us (4%)
    all_gather x1, waiting for transfers between devices, local(): lax.all_gather(pressure, 'mode', axis=0, tiled=True)  130 us
    pallas_call x1, Pallas kernels, vcycle(): pl.pallas_call(lambda *refs: cycle_kernel(geometry, *refs), out_shape=jax...  65.5 us
    dot_general x1, matrix products, local(): jnp.einsum('kij,jxn->kixn', own_rows, lax.all_gather(pressure, 'mode', ax...  13.7 us
    slice x8, local copies, waits for them, and re-layouts, along_last(): return jnp.concatenate([values[..., offset:], zeros], axis=-1)  13 us
    reduce_sum x1, other arithmetic, local(): jnp.sum(apply_operator(spread_faces, mixed_rim, 1.0, depth), axis=0)  9.84 us
    ppermute x2, starting transfers between devices, padded(): lax.ppermute(head, axis, [((i + 1) % count, i) for i in range(ends)])  8.67 us
    mul x5, local copies, waits for them, and re-layouts, apply_operator(): total = total + face * (values - other)  6.17 us
  transfers between devices with their start and end apart: 5, of which 3 were waited for; matrix products, arithmetic and copies ran while one was open for 10% of the time, Pallas kernels for 0%

profile of v1, /device:TPU:32, one launch (start us, length us, event | category | flops | bytes accessed | tf_op | source)
XLA Modules:
  0.0 301.3 jit_solution(5518988941868852522)
XLA Ops:
  7.2 2.3 reshape.47
  9.6 1.7 copy.21
  12.0 3.7 %collective-permute-start = (f32[13,1,4096]{2,0,1:T(8,128)S(1)}, f32[13,1,4096]{2,0,1:T(8,128)S(1)}, u32[]{:S(2)}, u32[]{:S(2)}) collective-permute-start(f32[13,1,4096]{2,0,1:T(8,128)S(1)} %get-tuple-element.13), channel_id=1, source_target_pairs={{8,0},{16,8},{24,16},{32,24},{40,32},{48,40},{56,48},{64,56},{72,6... | collective-permute-start | bytes 638984 | tf_op jit(solution)/shard_map/ppermute | solution.py:434
  15.7 1.9 collective-permute-start.1
  18.6 2.3 reshape.46
  21.5 1.6 fusion.57
  23.2 1.4 fusion.56
  27.6 1.2 copy.37
  28.9 1.3 copy.39
  38.6 130.4 %all-gather.2.cloned.1.call-done = f32[56,8,4096]{2,1,0:T(8,128)} async-done(((f32[7,8,4096]{2,1,0:T(8,128)}), f32[56,8,4096]{2,1,0:T(8,128)}) %all-gather.2.cloned.1.call-update) | async-done | bytes 7340048 | tf_op jit(solution)/shard_map/all_gather | solution.py:520
  169.0 13.7 %fusion = f32[5,7,8,4096]{3,1,2,0:T(8,128)S(1)} fusion(f32[56,8,4096]{2,1,0:T(8,128)} %all-gather.2.cloned.1.call-done, f32[56,5,56]{2,0,1:T(8,128)} %fusion.29, s32[]{:T(128)S(6)} %select_n.103), kind=kOutput, calls=%fused_computation | convolution fusion | flops 770703360 | bytes 11948036 | tf_op jit(solution)/shard_map/kij,jxn->kixn/dot_general | solution.py:517
  182.8 4.3 %fusion.52 = (f32[5,7,8,4095]{3,1,2,0:T(8,128)S(1)}, f32[5,7,8,4095]{3,1,2,0:T(8,128)}) fusion(f32[5,7,8,4096]{3,1,2,0:T(8,128)S(1)} %fusion), kind=kLoop, calls=%fused_computation.91 | loop fusion | bytes 18345600 | tf_op jit(solution)/shard_map/slice | solution.py:445
  187.0 2.6 copy.35
  189.6 2.0 fusion.53
  191.6 5.0 %collective-permute-start.2 = (f32[35,1,4096]{2,1,0:T(1,128)}, f32[35,1,4096]{2,1,0:T(1,128)}, u32[]{:S(2)}, u32[]{:S(2)}) collective-permute-start(f32[35,1,4096]{2,1,0:T(1,128)} %get-tuple-element.8), channel_id=1, source_target_pairs={{8,0},{16,8},{24,16},{32,24},{40,32},{48,40},{56,48},{64,56},{72,6... | collective-permute-start | bytes 1720328 | tf_op jit(solution)/shard_map/ppermute | solution.py:434
  196.7 2.3 collective-permute-start.3
  199.0 4.8 %fusion.51 = (f32[5,7,8,3968]{3,1,2,0:T(8,128)}, f32[5,7,8,3968]{3,1,2,0:T(8,128)}) fusion(f32[5,7,8,4096]{3,1,2,0:T(8,128)S(1)} %fusion), kind=kLoop, calls=%fused_computation.90 | loop fusion | bytes 17776640 | tf_op jit(solution)/shard_map/slice | solution.py:445
  204.2 1.4 copy.36
  205.6 4.5 %collective-permute-done.3 = f32[35,1,4096]{2,1,0:T(1,128)} collective-permute-done((f32[35,1,4096]{2,1,0:T(1,128)S(1)}, f32[35,1,4096]{2,1,0:T(1,128)}, u32[]{:S(2)}, u32[]{:S(2)}) %collective-permute-start.3) | collective-permute-done | bytes 573472 | tf_op jit(solution)/shard_map/ppermute | solution.py:432
  210.1 1.4 copy.38
  211.6 9.8 %fusion.10 = f32[7,8,4096]{2,0,1:T(8,128)S(1)} fusion(f32[5,7,8,4096]{3,1,2,0:T(8,128)S(1)} %fusion, f32[5,7,1,4096]{3,1,2,0:T(8,128)S(1)} %copy.38, f32[5,7,1,4096]{3,1,2,0:T(8,128)S(1)} %copy.36, f32[5,7,8,4095]{3,1,2,0:T(8,128)} %get-tuple-element.7, f32[5,7,8,4095]{3,1,2,0:T(8,128)S(1)} %get-tuple-element.6, f32[5,7,8,3968]{3,1,2,0:T(8,128)} %get-tuple-element.5, ...), kind=kLoop, calls=%fused_computation.11 | loop fusion | flops 25001984 | bytes 28653376 | tf_op jit(solution)/shard_map/reduce_sum | solution.py:525
  221.6 2.1 fusion.26
  225.7 65.5 %vcycle.1 = f32[7,256,128]{2,1,0:T(8,128)} custom-call(f32[7,256,128]{2,1,0:T(8,128)} %reshape_reshape.3.refs_0_, f32[1,256,128]{2,1,0:T(8,128)} %bitcast.67), custom_call_target="tpu_custom_call" | custom-call | tf_op jit(solution)/shard_map/vcycle/pallas_call | solution.py:411
  292.3 2.2 copy.72
  (78 shorter events, 17.3 us)
Async XLA Ops:
  7.2 161.8 %all-gather.2.cloned.1.call-start = ((), (), s32[]{:S(2)}) async-start(), calls=%async_computation | async-start | bytes 8257536 | tf_op jit(solution)/shard_map/all_gather | solution.py:520
  9.6 11.3 %copy-start.19 = (s32[4,210]{1,0:T(4,128)S(1)}, s32[4,210]{1,0:T(4,128)}, u32[]{:S(2)}) copy-start(s32[4,210]{1,0:T(4,128)} %param.7) | copy-start | bytes 10084
  12.0 13.5 %collective-permute-start = (f32[13,1,4096]{2,0,1:T(8,128)S(1)}, f32[13,1,4096]{2,0,1:T(8,128)S(1)}, u32[]{:S(2)}, u32[]{:S(2)}) collective-permute-start(f32[13,1,4096]{2,0,1:T(8,128)S(1)} %get-tuple-element.13), channel_id=1, source_target_pairs={{8,0},{16,8},{24,16},{32,24},{40,32},{48,40},{56,48},{64,56},{72,6... | collective-permute-start | bytes 638984 | tf_op jit(solution)/shard_map/ppermute | solution.py:434
  15.7 9.8 %collective-permute-start.1 = (f32[13,1,4096]{2,0,1:T(8,128)S(1)}, f32[13,1,4096]{2,0,1:T(8,128)S(1)}, u32[]{:S(2)}, u32[]{:S(2)}) collective-permute-start(f32[13,1,4096]{2,0,1:T(8,128)S(1)} %get-tuple-element.12), channel_id=1, source_target_pairs={{0,8},{8,16},{16,24},{24,32},{32,40},{40,48},{48,56},{56,64},{64,7... | collective-permute-start | bytes 638984 | tf_op jit(solution)/shard_map/ppermute | solution.py:432
  18.6 15.3 %copy-start = (f32[1,8,32,128]{3,2,1,0:T(8,128)}, f32[1,8,32,128]{3,2,1,0:T(8,128)S(1)}, u32[]{:S(2)}) copy-start(f32[1,8,32,128]{3,2,1,0:T(8,128)S(1)} %slice.143) | copy-start | bytes 393220
  25.5 8.3 %copy-start.9 = (f32[13,1,4096]{2,0,1:T(8,128)}, f32[13,1,4096]{2,0,1:T(8,128)S(1)}, u32[]{:S(2)}) copy-start(f32[13,1,4096]{2,0,1:T(8,128)S(1)} %collective-permute-done) | copy-start | bytes 638980
  25.5 8.3 %copy-start.11 = (f32[13,1,4096]{2,0,1:T(8,128)}, f32[13,1,4096]{2,0,1:T(8,128)S(1)}, u32[]{:S(2)}) copy-start(f32[13,1,4096]{2,0,1:T(8,128)S(1)} %collective-permute-done.1) | copy-start | bytes 638980
  191.6 12.5 %collective-permute-start.2 = (f32[35,1,4096]{2,1,0:T(1,128)}, f32[35,1,4096]{2,1,0:T(1,128)}, u32[]{:S(2)}, u32[]{:S(2)}) collective-permute-start(f32[35,1,4096]{2,1,0:T(1,128)} %get-tuple-element.8), channel_id=1, source_target_pairs={{8,0},{16,8},{24,16},{32,24},{40,32},{48,40},{56,48},{64,56},{72,6... | collective-permute-start | bytes 1720328 | tf_op jit(solution)/shard_map/ppermute | solution.py:434
  196.7 14.8 %copy-start.6 = (f32[5,8,4096]{2,1,0:T(8,128)S(1)}, f32[5,8,4096]{2,1,0:T(8,128)}, u32[]{:S(2)}) copy-start(f32[5,8,4096]{2,1,0:T(8,128)} %copy.37) | copy-start | bytes 1966084
  196.7 14.8 %copy-start.7 = (f32[5,8,4096]{2,1,0:T(8,128)S(1)}, f32[5,8,4096]{2,1,0:T(8,128)}, u32[]{:S(2)}) copy-start(f32[5,8,4096]{2,1,0:T(8,128)} %copy.39) | copy-start | bytes 1966084
  196.7 14.8 %copy-start.8 = (f32[5,8,4096]{2,1,0:T(8,128)S(1)}, f32[5,8,4096]{2,1,0:T(8,128)}, u32[]{:S(2)}) copy-start(f32[5,8,4096]{2,1,0:T(8,128)} %copy.40) | copy-start | bytes 1966084
  196.7 13.4 %collective-permute-start.3 = (f32[35,1,4096]{2,1,0:T(1,128)S(1)}, f32[35,1,4096]{2,1,0:T(1,128)}, u32[]{:S(2)}, u32[]{:S(2)}) collective-permute-start(f32[35,1,4096]{2,1,0:T(1,128)S(1)} %get-tuple-element.9), channel_id=1, source_target_pairs={{0,8},{8,16},{16,24},{24,32},{32,40},{40,48},{48,56},{56,64},{64,7... | collective-permute-start | bytes 1720328 | tf_op jit(solution)/shard_map/ppermute | solution.py:432
  211.5 10.0 %copy-start.1 = (f32[7,8,4095]{2,0,1:T(8,128)S(1)}, f32[7,8,4095]{2,0,1:T(8,128)}, u32[]{:S(2)}) copy-start(f32[7,8,4095]{2,0,1:T(8,128)} %get-tuple-element.26) | copy-start | bytes 2751844
  211.5 10.0 %copy-start.2 = (f32[7,8,4095]{2,0,1:T(8,128)S(1)}, f32[7,8,4095]{2,0,1:T(8,128)}, u32[]{:S(2)}) copy-start(f32[7,8,4095]{2,0,1:T(8,128)} %get-tuple-element.27) | copy-start | bytes 2751844
  211.5 10.0 %copy-start.3 = (f32[7,8,3968]{2,0,1:T(8,128)S(1)}, f32[7,8,3968]{2,0,1:T(8,128)}, u32[]{:S(2)}) copy-start(f32[7,8,3968]{2,0,1:T(8,128)} %get-tuple-element.24) | copy-start | bytes 2666500
  211.5 10.0 %copy-start.4 = (f32[7,8,3968]{2,0,1:T(8,128)S(1)}, f32[7,8,3968]{2,0,1:T(8,128)}, u32[]{:S(2)}) copy-start(f32[7,8,3968]{2,0,1:T(8,128)} %get-tuple-element.25) | copy-start | bytes 2666500
  211.5 10.0 %copy-start.5 = (f32[7,8,4096]{2,1,0:T(8,128)S(1)}, f32[7,8,4096]{2,1,0:T(8,128)}, u32[]{:S(2)}) copy-start(f32[7,8,4096]{2,1,0:T(8,128)} %reshape.46) | copy-start | bytes 2752516
  211.5 10.0 %copy-start.10 = (f32[13,1,4096]{2,0,1:T(8,128)S(1)}, f32[13,1,4096]{2,0,1:T(8,128)}, u32[]{:S(2)}) copy-start(f32[13,1,4096]{2,0,1:T(8,128)} %copy-done.9) | copy-start | bytes 638980
  211.6 10.0 %copy-start.12 = (f32[13,1,4096]{2,0,1:T(8,128)S(1)}, f32[13,1,4096]{2,0,1:T(8,128)}, u32[]{:S(2)}) copy-start(f32[13,1,4096]{2,0,1:T(8,128)} %copy-done.11) | copy-start | bytes 638980
  211.6 10.0 %copy-start.14 = (f32[1,8,4096]{2,1,0:T(8,128)S(1)}, f32[1,8,4096]{2,1,0:T(8,128)}, u32[]{:S(2)}) copy-start(f32[1,8,4096]{2,1,0:T(8,128)} %copy.66) | copy-start | bytes 393220
  211.6 10.0 %copy-start.15 = (f32[1,8,4096]{2,1,0:T(8,128)S(1)}, f32[1,8,4096]{2,1,0:T(8,128)}, u32[]{:S(2)}) copy-start(f32[1,8,4096]{2,1,0:T(8,128)} %copy.67) | copy-start | bytes 393220
  211.6 10.0 %copy-start.16 = (f32[1,8,4096]{2,1,0:T(8,128)S(1)}, f32[1,8,4096]{2,1,0:T(8,128)}, u32[]{:S(2)}) copy-start(f32[1,8,4096]{2,1,0:T(8,128)} %copy.68) | copy-start | bytes 393220
  211.6 10.0 %copy-start.17 = (f32[1,8,4096]{2,1,0:T(8,128)S(1)}, f32[1,8,4096]{2,1,0:T(8,128)}, u32[]{:S(2)}) copy-start(f32[1,8,4096]{2,1,0:T(8,128)} %copy.69) | copy-start | bytes 393220
  211.6 10.0 %copy-start.18 = (f32[1,8,4096]{2,1,0:T(8,128)S(1)}, f32[1,8,4096]{2,1,0:T(8,128)}, u32[]{:S(2)}) copy-start(f32[1,8,4096]{2,1,0:T(8,128)} %copy.70) | copy-start | bytes 393220
  (1 other events, 4.2 us)
Sparse Core Ops, SparseCore 0:
  11.2 157.7 all-gather.1

commit v2 on v1

--- a/solution.py
+++ b/solution.py
@@ -9,6 +9,8 @@
 F32 = jnp.float32
 P_SIZE = 56
 KL = 5
+RING = 4
+CHUNKS = ((7, 1), (0, 1), (1, 2), (5, 2), (3, 2))
 SWEEPS = 2
 COARSE = 8
 LEVELS = 4
@@ -139,12 +141,15 @@
 
 
 def cycle_kernel(
-    geometry, b_ref, field_ref, out_ref,
+    geometry, place_ref, share_ref, p_ref, source_ref, field_ref, out_ref, residual_ref,
     c0, w0, i0, g0, b0, s0, a0, d0,
     c1, w1, i1, g1, b1, s1, a1, d1,
     c2, w2, i2, g2, b2, s2, a2, d2,
     c3, w3, i3, g3, b3, s3, a3, d3,
-    temp, line, sums, send_sem, recv_sem,
+    temp, line, sums,
+    q0, q1, q2, q3, q4, rim_low, rim_high, spread_fields, face_x, face_y, face_z,
+    mix_a, mix_b, mix_c, mix_d, mix_e, mix_f, hold_a, hold_b, hold_c, partial, arriving,
+    send_sem, recv_sem,
 ):
     modes, width, rows, blocks = geometry
     grid = width * blocks
@@ -156,12 +161,12 @@
     cols = blocks // ROW
     counter = [0]
 
-    def start_copy(src, dst, target, exists=None):
+    def start_copy(src, dst, target, exists=None, other_mode=None):
         number = counter[0]
         counter[0] += 1
         copy = pltpu.make_async_remote_copy(
             src_ref=src, dst_ref=dst, send_sem=send_sem.at[number], recv_sem=recv_sem.at[number],
-            device_id=(target, mode), device_id_type=MESH,
+            device_id=(target, mode if other_mode is None else other_mode), device_id_type=MESH,
         )
         if exists is None:
             copy.start()
@@ -192,8 +197,21 @@
     def col_peer(q):
         return ((col_at + q) % cols) * ROW + row_at
 
-    for ref in (c0, b0, s0, a0, d0, c1, b1, s1, a1, d1, c2, b2, s2, a2, d2, c3, b3, s3, a3, d3):
+    own0 = PAD + 4 * rows
+    size0 = width * rows
+    for ref in (c0, c1, b1):
         zero_all(ref)
+    for at in (pl.ds(own0 - 3 * rows, 3 * rows), pl.ds(own0 + size0, 3 * rows)):
+        b0[:, at, :] = jnp.zeros((b0.shape[0], 3 * rows, LANES), F32)
+    spread_fields[...] = jnp.zeros(spread_fields.shape, F32)
+
+    @pl.when(me == 0)
+    def _():
+        zero_all(rim_low)
+
+    @pl.when(me == blocks - 1)
+    def _():
+        zero_all(rim_high)
 
     barrier = pltpu.get_barrier_semaphore()
     expected = ROW - 1 + cols - 1
@@ -206,19 +224,198 @@
         pl.semaphore_signal(barrier, inc=1, device_id=(row_peer(q), mode), device_id_type=MESH)
     for q in range(1, cols):
         pl.semaphore_signal(barrier, inc=1, device_id=(col_peer(q), mode), device_id_type=MESH)
+    y = mode // 2
+    partner = y * 2 + 1 - mode % 2
+    up, down = (mode + 2) % (2 * RING), (mode + 2 * RING - 2) % (2 * RING)
+    for other in (up, down, partner):
+        pl.semaphore_signal(barrier, inc=1, device_id=(me, other), device_id_type=MESH)
+    expected = expected + 3
+    own_slot = pl.ds(y * modes, modes)
+    parts = (q0, q1, q2, q3, q4)
+    for (plane, count), part in zip(CHUNKS, parts):
+        for m in range(modes):
+            part[y * modes + m] = p_ref[m, pl.ds(plane * rows, count * rows), :]
     pl.semaphore_wait(barrier, expected)
 
-    own0 = PAD + 4 * rows
-    size0 = width * rows
-    halos = []
-    halos.append(to_neighbour(b_ref.at[:, pl.ds(size0 - 3 * rows, 3 * rows)], b0.at[pl.ds(0, modes), pl.ds(own0 - 3 * rows, 3 * rows)], 1))
-    halos.append(to_neighbour(b_ref.at[:, pl.ds(0, 3 * rows)], b0.at[pl.ds(0, modes), pl.ds(own0 + size0, 3 * rows)], -1))
+    def slot(distance, first=0, count=modes):
+        return pl.ds((y + RING + distance) % RING * modes + first, count)
+
+    near, far = {}, {}
+
+    def send_own(c):
+        plane, count = CHUNKS[c]
+        src = p_ref.at[:, pl.ds(plane * rows, count * rows)]
+        dst = parts[c].at[own_slot]
+        near[c] = (start_copy(src, dst, me, None, up), start_copy(src, dst, me, None, down))
+        sends.extend((copy, None) for copy in near[c])
+
+    def pass_on(c):
+        cut = modes // 2 + (c + 1) % 2
+        near[c][0].wait_recv()
+        at = parts[c].at[slot(-1, 0, cut)]
+        first = start_copy(at, at, me, None, up)
+        near[c][1].wait_recv()
+        at = parts[c].at[slot(1, cut, modes - cut)]
+        far[c] = (first, start_copy(at, at, me, None, down))
+        sends.extend((copy, None) for copy in far[c])
+
+    def complete(c):
+        far[c][0].wait_recv()
+        far[c][1].wait_recv()
+
+    send_own(0)
+    send_own(1)
+
     c_halos = []
     c_halos.append(to_neighbour(field_ref.at[0, pl.ds(size0 - 4 * rows, 4 * rows)], c0.at[pl.ds(own0 - 4 * rows, 4 * rows)], 1))
     c_halos.append(to_neighbour(field_ref.at[0, pl.ds(0, 4 * rows)], c0.at[pl.ds(own0 + size0, 4 * rows)], -1))
+    own_f = PAD + rows
+    c_halos.append(to_neighbour(field_ref.at[pl.ds(1, KL), pl.ds(size0 - rows, rows)], spread_fields.at[:, pl.ds(PAD, rows)], 1))
+    c_halos.append(to_neighbour(field_ref.at[pl.ds(1, KL), pl.ds(0, rows)], spread_fields.at[:, pl.ds(own_f + size0, rows)], -1))
     c0[pl.ds(own0, size0), :] = field_ref[0]
-    for m in range(modes):
-        b0[m, pl.ds(own0, size0), :] = b_ref[m]
+    for k in range(KL):
+        spread_fields[k, pl.ds(own_f, size0), :] = field_ref[k + 1]
+    for mix in (mix_a, mix_b, mix_c, mix_d, mix_e, mix_f):
+        mix[:, pl.ds(rows, 8), :] = jnp.zeros((mix.shape[0], 8, LANES), F32)
+    for pair in c_halos:
+        arrived(pair)
+
+    @pl.loop(0, width + 1)
+    def _(turn):
+        lane = lax.broadcasted_iota(jnp.int32, (rows, LANES), 1)
+        line_at = lax.broadcasted_iota(jnp.int32, (rows, LANES), 0)
+        base = pl.multiple_of(turn * rows, 8)
+        for k in range(KL + 1):
+            ref = c0 if k == 0 else spread_fields.at[k - 1]
+            shift = own0 - rows if k == 0 else PAD
+            here = ref[pl.ds(shift + base, rows), :]
+            face_x[k, pl.ds(base, rows), :] = 0.5 * (here + ref[pl.ds(shift + base + rows, rows), :])
+            face_y[k, pl.ds(base, rows), :] = jnp.where(
+                line_at < rows - 1, 0.5 * (here + ref[pl.ds(shift + base + 1, rows), :]), 0.0)
+            face_z[k, pl.ds(base, rows), :] = jnp.where(
+                lane < LANES - 1, 0.5 * (here + pltpu.roll(here, LANES - 1, 1)), 0.0)
+
+    def source_of(x):
+        if x < 0:
+            return rim_low, 0
+        if x >= width:
+            return rim_high, 0
+        for (plane, count), part in zip(CHUNKS, parts):
+            if plane <= x < plane + count:
+                return part, (x - plane) * rows
+
+    def mixed(t, k, x):
+        ref, at = source_of(x)
+        entry = t * KL + k
+        return (
+            share_ref[0, entry] * ref[place_ref[0, entry], pl.ds(at, rows), :]
+            + share_ref[1, entry] * ref[place_ref[1, entry], pl.ds(at, rows), :]
+        )
+
+    def fill(first, fields, now, x):
+        @pl.loop(0, modes)
+        def _(t):
+            for k in range(KL):
+                now[t * fields + k, pl.ds(0, rows), :] = mixed(first + t, k, x)
+            if fields > KL:
+                ref, at = source_of(x)
+                now[t * fields + KL, pl.ds(0, rows), :] = ref[y * modes + t, pl.ds(at, rows), :]
+
+    def advance(first, fields, now, later, hold, x, emit):
+        here = pl.ds((x + 1) * rows, rows)
+
+        @pl.loop(0, modes)
+        def _(t):
+            along_x = jnp.zeros((rows, LANES), F32)
+            along_y, along_z = along_x, along_x
+            for k in range(fields):
+                if k < KL:
+                    field = k + 1
+                    value = mixed(first + t, k, x + 1)
+                else:
+                    field = 0
+                    ref, at = source_of(x + 1)
+                    value = ref[y * modes + t, pl.ds(at, rows), :]
+                at = t * fields + k
+                later[at, pl.ds(0, rows), :] = value
+                old = now[at, pl.ds(0, rows), :]
+                along_x = along_x + face_x[field, here, :] * (old - value)
+                if emit is not None:
+                    along_y = along_y + face_y[field, here, :] * (old - now[at, pl.ds(1, rows), :])
+                    along_z = along_z + face_z[field, here, :] * (old - pltpu.roll(old, LANES - 1, 1))
+            if emit is not None:
+                emit(t, along_x - hold[t] + (along_y - pltpu.roll(along_y, 1, 0))
+                     + (along_z - pltpu.roll(along_z, 1, 1)))
+            hold[t] = along_x
+
+    to_partner = {}
+
+    def send_partner(x):
+        to_partner[x] = start_copy(partial.at[x], arriving.at[x], me, None, partner)
+        sends.append((to_partner[x], None))
+
+    def emit_partner(x):
+        def emit(t, value):
+            partial[x, t] = value
+        return emit
+
+    def emit_own(x):
+        def emit(t, value):
+            at = pl.ds(own0 + x * rows, rows)
+            b0[t, at, :] = source_ref[t, pl.ds(x * rows, rows), :] - value
+        return emit
+
+    def partner_step(now, later, hold, x, emits=True):
+        advance(modes, KL, now, later, hold, x, emit_partner(x) if emits else None)
+
+    last = width - 1
+    pass_on(0)
+    send_own(2)
+    pass_on(1)
+    send_own(3)
+    complete(0)
+    low = to_neighbour(q0, rim_low, 1)
+    complete(1)
+    high = to_neighbour(q1, rim_high, -1)
+    pass_on(2)
+    send_own(4)
+    complete(2)
+    arrived(low)
+    fill(modes, KL, mix_a, -1)
+    partner_step(mix_a, mix_b, hold_a, -1, False)
+    partner_step(mix_b, mix_a, hold_a, 0)
+    send_partner(0)
+    pass_on(3)
+    partner_step(mix_a, mix_b, hold_a, 1)
+    send_partner(1)
+    complete(3)
+    arrived(high)
+    fill(modes, KL, mix_c, 5)
+    partner_step(mix_c, mix_d, hold_b, 5, False)
+    partner_step(mix_d, mix_c, hold_b, 6)
+    send_partner(6)
+    pass_on(4)
+    partner_step(mix_c, mix_d, hold_b, 7)
+    send_partner(7)
+    complete(4)
+    partner_step(mix_b, mix_a, hold_a, 2)
+    send_partner(2)
+    partner_step(mix_a, mix_b, hold_a, 3)
+    partner_step(mix_b, mix_a, hold_a, 4)
+    partner_step(mix_a, mix_b, hold_a, 5)
+    send_partner(5)
+    send_partner(3)
+    send_partner(4)
+    fill(0, KL + 1, mix_e, -1)
+    now, later = mix_e, mix_f
+    for x in range(-1, width):
+        advance(0, KL + 1, now, later, hold_c, x, emit_own(x) if x >= 0 else None)
+        now, later = later, now
+    for ref in (s0, a0, d0, s1, a1, d1, s2, a2, d2, s3, a3, d3):
+        zero_all(ref)
+    for ref in (c2, c3):
+        ref[pl.ds(0, PAD), :] = jnp.zeros((PAD, LANES), F32)
+        ref[pl.ds(ref.shape[0] - PAD, PAD), :] = jnp.zeros((PAD, LANES), F32)
 
     merge = pairing()
     spread = spreading()
@@ -244,8 +441,6 @@
         sends.append((copy, None))
         c2_row.append((copy, None))
 
-    for pair in c_halos:
-        arrived(pair)
     level_faces(c0, g0, w0, i0, PAD + rows, (width + 6) * rows, 16, rows, LANES, 1.0, me * width - 4, grid)
 
     for pair in c2_row:
@@ -295,6 +490,23 @@
         line[1, pl.ds(x, 1), :] = inv
         line[2, pl.ds(x, 1), :] = ratio
 
+    def receive(x):
+        to_partner[x].wait_recv()
+        at = pl.ds(own0 + x * rows, rows)
+        for m in range(modes):
+            value = b0[m, at, :] - arriving[x, m]
+            b0[m, at, :] = value
+            residual_ref[m, pl.ds(x * rows, rows), :] = value
+
+    halos = []
+    for x in (0, 1, 2):
+        receive(x)
+    halos.append(to_neighbour(b0.at[pl.ds(0, modes), pl.ds(own0, 3 * rows)], b0.at[pl.ds(0, modes), pl.ds(own0 + size0, 3 * rows)], -1))
+    for x in (6, 7, 5):
+        receive(x)
+    halos.append(to_neighbour(b0.at[pl.ds(0, modes), pl.ds(own0 + size0 - 3 * rows, 3 * rows)], b0.at[pl.ds(0, modes), pl.ds(own0 - 3 * rows, 3 * rows)], 1))
+    for x in (3, 4):
+        receive(x)
     for pair in halos:
         arrived(pair)
     first_sweep(s0, b0, w0, modes, PAD + rows, (width + 6) * rows, 16)
@@ -384,8 +596,28 @@
             pl.when(exists)(copy.wait_send)
 
 
-def vcycle(residual, fields, blocks):
-    modes, width, rows, depth = residual.shape
+def coupling_places(coupling_list, mode, modes):
+    side = mode % 2
+    targets = jnp.concatenate([
+        mode * modes + jnp.arange(modes, dtype=jnp.int32),
+        (mode + 1 - 2 * side) * modes + jnp.arange(modes, dtype=jnp.int32),
+    ])
+    wanted = (targets[:, None] * 8 + jnp.arange(1, KL + 1, dtype=jnp.int32)[None, :]).reshape(-1)
+    given = coupling_list[0] * 8 + coupling_list[2]
+    other = coupling_list[1]
+    held = (other // modes) % 2 == side
+    slot = other // (2 * modes) * modes + other % modes
+    match = jnp.logical_and(wanted[:, None] == given[None, :], held[None, :])
+    code = jnp.where(match, slot * 4 + coupling_list[3], -1)
+    high = jnp.max(code, axis=1)
+    low = jnp.min(jnp.where(match, slot * 4 + coupling_list[3], 1 << 20), axis=1)
+    low = jnp.where(low < high, low, 0)
+    both = jnp.maximum(jnp.stack([high, low]), 0)
+    return both // 4, jnp.sqrt((both % 4).astype(F32))
+
+
+def local(blocks, pressure, source, kl_field, coupling_list):
+    modes, width, rows, depth = pressure.shape
     plane = width * rows
     even = modes + modes % 2
     r1, r2, r3 = rows // 2, rows // 4, rows // 8
@@ -399,134 +631,38 @@
         scratch += [pltpu.VMEM((size, LANES), F32)] * 3
         scratch += [pltpu.VMEM((6, size, LANES), F32)]
         scratch += [pltpu.VMEM((count, size, LANES), F32)] * 4
-    copies = 4 + 4 + 2 + 2 * (ROW - 1 + blocks // ROW - 1)
+    cycle_copies = 4 + 4 + 2 + 2 * (ROW - 1 + blocks // ROW - 1)
+    copies = cycle_copies + 4 * len(CHUNKS) + 4 + width
+    held = RING * modes
     scratch += [
         pltpu.VMEM((grid // 4 * r2, LANES), F32),
         pltpu.VMEM((3, grid // 8, LANES), F32),
         pltpu.VMEM((grid // 8, LANES), F32),
-        pltpu.SemaphoreType.DMA((copies,)),
-        pltpu.SemaphoreType.DMA((copies,)),
     ]
+    scratch += [pltpu.VMEM((held, count * rows, LANES), F32) for _, count in CHUNKS]
+    scratch += [pltpu.VMEM((held, rows, LANES), F32)] * 2
+    scratch += [pltpu.VMEM((KL, (width + 2) * rows + 2 * PAD, LANES), F32)]
+    scratch += [pltpu.VMEM((KL + 1, (width + 1) * rows, LANES), F32)] * 3
+    scratch += [pltpu.VMEM((modes * KL, rows + 8, LANES), F32)] * 4
+    scratch += [pltpu.VMEM((modes * (KL + 1), rows + 8, LANES), F32)] * 2
+    scratch += [pltpu.VMEM((modes, rows, LANES), F32)] * 3
+    scratch += [pltpu.VMEM((width, modes, rows, LANES), F32)] * 2
+    scratch += [pltpu.SemaphoreType.DMA((copies,))] * 2
     geometry = (modes, width, rows, blocks)
-    out = pl.pallas_call(
+    places, shares = coupling_places(coupling_list, lax.axis_index("mode"), modes)
+    shape = jax.ShapeDtypeStruct((modes, plane, depth), F32)
+    out, residual = pl.pallas_call(
         lambda *refs: cycle_kernel(geometry, *refs),
-        out_shape=jax.ShapeDtypeStruct((modes, plane, depth), F32),
-        in_specs=[pl.BlockSpec(memory_space=pltpu.VMEM)] * 2,
-        out_specs=pl.BlockSpec(memory_space=pltpu.VMEM),
+        out_shape=(shape, shape),
+        in_specs=[pl.BlockSpec(memory_space=pltpu.SMEM)] * 2 + [pl.BlockSpec(memory_space=pltpu.VMEM)] * 3,
+        out_specs=[pl.BlockSpec(memory_space=pltpu.VMEM)] * 2,
         scratch_shapes=scratch,
         compiler_params=pltpu.CompilerParams(
-            collective_id=1, has_side_effects=True, vmem_limit_bytes=56 * 2**20),
-        name="vcycle",
-    )(residual.reshape(modes, plane, depth), fields[0:1].reshape(1, plane, depth))
-    return out.reshape(residual.shape)
-
-
-def padded(cells, sides, width):
-    for axis, dim in sides:
-        count = lax.axis_size(axis)
-        ends = count - 1
-        head = lax.slice_in_dim(cells, 0, width, axis=dim)
-        tail = lax.slice_in_dim(cells, cells.shape[dim] - width, cells.shape[dim], axis=dim)
-        cells = jnp.concatenate(
-            [
-                lax.ppermute(tail, axis, [(i, (i + 1) % count) for i in range(ends)]),
-                cells,
-                lax.ppermute(head, axis, [((i + 1) % count, i) for i in range(ends)]),
-            ],
-            axis=dim,
-        )
-    return cells
-
-
-def along_last(values, offset):
-    size = values.shape[-1]
-    zeros = jnp.zeros(values.shape[:-1] + (abs(offset),), values.dtype)
-    if offset > 0:
-        return jnp.concatenate([values[..., offset:], zeros], axis=-1)
-    return jnp.concatenate([zeros, values[..., : size + offset]], axis=-1)
-
-
-def neighbours(values_rim, depth):
-    values = values_rim[..., 1:-1, :]
-    positions = lax.iota(jnp.int32, values.shape[-1]) % depth
-    upper = positions < depth - 1
-    lower = positions > 0
-    others = (
-        values_rim[..., 2:, :],
-        values_rim[..., :-2, :],
-        along_last(values, depth),
-        along_last(values, -depth),
-        jnp.where(upper, along_last(values, 1), 0.0),
-        jnp.where(lower, along_last(values, -1), 0.0),
-    )
-    return (values, others)
-
-
-def faces_of(field_rim, depth):
-    field, others = neighbours(field_rim, depth)
-    plane = field.shape[-1]
-    places = lax.iota(jnp.int32, plane)
-    within = places % depth
-    inside = (places < plane - depth, places >= depth, within < depth - 1, within > 0)
-    collected = [0.5 * (field + others[0]), 0.5 * (field + others[1])]
-    for keep, other in zip(inside, others[2:]):
-        collected.append(jnp.where(keep, 0.5 * (field + other), 0.0))
-    return collected
-
-
-def apply_operator(faces, values_rim, scale, depth):
-    values, others = neighbours(values_rim, depth)
-    total = faces[0] * (values - others[0])
-    for face, other in zip(faces[1:], others[1:]):
-        total = total + face * (values - other)
-    return scale * total
-
-
-def diagonal_of(faces, scale):
-    total = faces[0]
-    for face in faces[1:]:
-        total = total + face
-    return scale * total
-
-
-def coupling_tables(coupling_list):
-    modes = jnp.arange(P_SIZE, dtype=jnp.int32)
-    orders = jnp.arange(1, KL + 1, dtype=jnp.int32)
-    firsts = (coupling_list[0][:, None] == modes[None, :]).astype(jnp.float32)
-    seconds = (coupling_list[1][:, None] == modes[None, :]).astype(jnp.float32)
-    weights = jnp.sqrt(coupling_list[3].astype(jnp.float32))
-    which = (coupling_list[2][:, None] == orders[None, :]).astype(jnp.float32) * weights[:, None]
-    return jnp.einsum("nk,ni,nj->kij", which, firsts, seconds, precision=lax.Precision.HIGHEST)
-
-
-def local(blocks, pressure, source, kl_field, coupling_list):
-    local_modes, width, rows, depth = pressure.shape
-    plane = rows * depth
-    pressure = pressure.reshape(local_modes, width, plane)
-    source = source.reshape(local_modes, width, plane)
-    fields = kl_field.reshape(kl_field.shape[0], width, plane)
-    joined = padded(jnp.concatenate([pressure, fields], axis=0), (("space", 1),), 1)
-    pressure_rim = joined[:local_modes]
-    field_rim = joined[local_modes:]
-    mean_faces = faces_of(field_rim[0:1], depth)
-    spread_faces = faces_of(field_rim[1:, None], depth)
-    image = apply_operator(mean_faces, pressure_rim, 1.0, depth)
-    tables = coupling_tables(coupling_list)
-    first = lax.axis_index("mode") * local_modes
-    own_rows = lax.dynamic_slice_in_dim(tables, first, local_modes, axis=1)
-    mixed = jnp.einsum(
-        "kij,jxn->kixn",
-        own_rows,
-        lax.all_gather(pressure, "mode", axis=0, tiled=True),
-        precision=lax.Precision.HIGHEST,
-    )
-    mixed_rim = padded(mixed.reshape(KL * local_modes, width, plane), (("space", 1),), 1)
-    mixed_rim = mixed_rim.reshape(KL, local_modes, width + 2, plane)
-    coupled = jnp.sum(apply_operator(spread_faces, mixed_rim, 1.0, depth), axis=0)
-    residual = source - (image + coupled)
-    shape = (local_modes, width, rows, depth)
-    residual = residual.reshape(shape)
-    return (vcycle(residual, kl_field, blocks), residual)
+            collective_id=1, has_side_effects=True, vmem_limit_bytes=60 * 2**20),
+        name="coupled_cycle",
+    )(places, shares, pressure.reshape(modes, plane, depth), source.reshape(modes, plane, depth),
+      kl_field.reshape(KL + 1, plane, depth))
+    return (out.reshape(pressure.shape), residual.reshape(pressure.shape))
 
 
 def solution(mesh):

time: 302 us -> 141 us (0.47)
  waiting for transfers between devices: 135 us -> 0 us
  Pallas kernels: 65.5 us -> 135 us
  local copies, waits for them, and re-layouts: 44 us -> 3.88 us
  matrix products: 14.7 us -> 0 us
  between operations: 14.5 us -> 0.7 us
  starting transfers between devices: 12.9 us -> 0 us
  other arithmetic: 14.4 us -> 1.59 us
    all_gather x1 -> x0, waiting for transfers between devices: 130 us -> none  [local(): lax.all_gather(pressure, 'mode', axis=0, tiled=True)]
    pallas_call x1, Pallas kernels: 65.5 us -> 135 us  [local(): pl.pallas_call(lambda *refs: cycle_kernel(geometry, *refs), out_shape=(sh...]
    slice x11 -> x0, local copies, waits for them, and re-layouts: 16 us -> none  [the longest x8 13 us: along_last(): return jnp.concatenate([values[..., offset:], zeros], axis=-1)]
    dot_general x2 -> x0, matrix products: 14.7 us -> none  [the longest x1 13.7 us: local(): jnp.einsum('kij,jxn->kixn', own_rows, lax.all_gather(pressure, 'mode', ax...]
    ppermute x4 -> x0, starting transfers between devices: 12.9 us -> none  [the longest x2 8.67 us: padded(): lax.ppermute(head, axis, [((i + 1) % count, i) for i in range(ends)])]
    reduce_sum x1 -> x0, other arithmetic: 9.84 us -> none  [local(): jnp.sum(apply_operator(spread_faces, mixed_rim, 1.0, depth), axis=0)]
    reshape x7 -> x0, local copies, waits for them, and re-layouts: 8.48 us -> none  [the longest x2 4.06 us: local(): pressure = pressure.reshape(local_modes, width, plane)]
    mul x6 -> x0, local copies, waits for them, and re-layouts: 6.55 us -> none  [the longest x5 6.17 us: apply_operator(): total = total + face * (values - other)]
  transfers between devices with their start and end apart: 5 -> 0, of which waited for: 3 -> 0; matrix products, arithmetic and copies ran while one was open for 10% -> 0% of each run, Pallas kernels for 0% -> 0%
where the time goes in v2:
time: 141 us
  Pallas kernels  135 us (96%)
  local copies, waits for them, and re-layouts  3.88 us (3%)
  other arithmetic  1.59 us (1%)
    pallas_call x1, Pallas kernels, local(): pl.pallas_call(lambda *refs: cycle_kernel(geometry, *refs), out_shape=(sh...  135 us
    unnamed x6, local copies, waits for them, and re-layouts  3.79 us

profile of v2, /device:TPU:32, one launch (start us, length us, event | category | flops | bytes accessed | tf_op | source)
XLA Modules:
  0.0 140.7 jit_solution(7171756125773712214)
XLA Ops:
  0.7 0.0 copy-start.1
  0.7 0.1 add_multiply_fusion
  0.7 0.6 copy-done.1
  1.4 0.1 broadcast_add_fusion
  1.5 0.1 add.92
  1.6 0.2 select_reduce_fusion.1
  1.8 0.6 and_select_fusion.3.refs_0_
  2.4 0.6 fusion.3.refs_1_
  3.0 134.5 %coupled_cycle.1 = (f32[7,256,128]{2,1,0:T(8,128)}, f32[7,256,128]{2,1,0:T(8,128)}) custom-call(s32[2,70]{1,0:T(2,128)} %and_select_fusion.3.refs_0_, f32[2,70]{1,0:T(2,128)} %fusion.3.refs_1_, f32[7,256,128]{2,1,0:T(8,128)} %bitcast.15, f32[7,256,128]{2,1,0:T(8,128)} %bitcast.16, f32[6,256,128]{2,1,0:T(8,128)} %bitcast.17), custom_call_target="tpu_custom_call" | custom-call | tf_op jit(solution)/shard_map/coupled_cycle/pallas_call | solution.py:654
  137.5 0.0 copy-start
  137.5 2.3 %copy.8 = f32[7,8,32,128]{3,2,1,0:T(8,128)} copy(f32[7,8,32,128]{3,2,1,0:T(8,128)} %bitcast.14) | data formatting | bytes 1835008
  139.7 0.0 copy-done
  139.7 0.9 copy.9
  (6 shorter events, 0.1 us)
Async XLA Ops:
  0.7 0.7 copy-start.1
  137.5 2.3 %copy-start = (f32[7,256,128]{2,1,0:T(8,128)S(1)}, f32[7,256,128]{2,1,0:T(8,128)}, u32[]{:S(2)}) copy-start(f32[7,256,128]{2,1,0:T(8,128)} %get-tuple-element.5) | copy-start | bytes 2752516

commit v3 on v2

--- a/solution.py
+++ b/solution.py
@@ -10,7 +10,9 @@
 P_SIZE = 56
 KL = 5
 RING = 4
-CHUNKS = ((7, 1), (0, 1), (1, 2), (5, 2), (3, 2))
+CHUNKS = ((7, 1), (0, 1), (1, 1), (2, 1), (6, 1), (5, 1), (3, 1), (4, 1))
+COPIES = 96
+NEAR = (1, -1, 2, -2, 3, -3)
 SWEEPS = 2
 COARSE = 8
 LEVELS = 4
@@ -118,10 +120,10 @@
     return 0.125 * split_dot(jnp.concatenate([left, right], axis=-1), matrix)
 
 
-def prolong(fine, modes, fine_first, coarse, coarse_first, planes, rows, matrix, temp):
+def prolong(fine, modes, fine_first, coarse, planes, rows, matrix, temp):
     count = planes * rows
     for p in range((modes + 1) // 2):
-        both = split_dot(coarse[p, pl.ds(coarse_first, count), :], matrix)
+        both = split_dot(coarse(p), matrix)
         for part in range(2):
             m = 2 * p + part
             if m >= modes:
@@ -147,7 +149,7 @@
     c2, w2, i2, g2, b2, s2, a2, d2,
     c3, w3, i3, g3, b3, s3, a3, d3,
     temp, line, sums,
-    q0, q1, q2, q3, q4, rim_low, rim_high, spread_fields, face_x, face_y, face_z,
+    small, slots, q0, q1, q2, q3, q4, q5, q6, q7, rim_low, rim_high, spread_fields, face_x, face_y, face_z,
     mix_a, mix_b, mix_c, mix_d, mix_e, mix_f, hold_a, hold_b, hold_c, partial, arriving,
     send_sem, recv_sem,
 ):
@@ -174,6 +176,15 @@
             pl.when(exists)(copy.start)
         return copy
 
+    def finish():
+        for m in range(modes):
+            out_ref[m] = a0[m, pl.ds(own0, size0), :]
+        for copy, exists in sends:
+            if exists is None:
+                copy.wait_send()
+            else:
+                pl.when(exists)(copy.wait_send)
+
     def shift_exists(delta):
         return me + delta < blocks if delta > 0 else me + delta >= 0
 
@@ -199,7 +210,7 @@
 
     own0 = PAD + 4 * rows
     size0 = width * rows
-    for ref in (c0, c1, b1):
+    for ref in (c0, c1, b1, c2, b2, c3):
         zero_all(ref)
     for at in (pl.ds(own0 - 3 * rows, 3 * rows), pl.ds(own0 + size0, 3 * rows)):
         b0[:, at, :] = jnp.zeros((b0.shape[0], 3 * rows, LANES), F32)
@@ -215,7 +226,7 @@
 
     barrier = pltpu.get_barrier_semaphore()
     expected = ROW - 1 + cols - 1
-    for delta in (1, -1, 2, -2):
+    for delta in NEAR:
         @pl.when(shift_exists(delta))
         def _():
             pl.semaphore_signal(barrier, inc=1, device_id=(me + delta, mode), device_id_type=MESH)
@@ -231,7 +242,7 @@
         pl.semaphore_signal(barrier, inc=1, device_id=(me, other), device_id_type=MESH)
     expected = expected + 3
     own_slot = pl.ds(y * modes, modes)
-    parts = (q0, q1, q2, q3, q4)
+    parts = (q0, q1, q2, q3, q4, q5, q6, q7)
     for (plane, count), part in zip(CHUNKS, parts):
         for m in range(modes):
             part[y * modes + m] = p_ref[m, pl.ds(plane * rows, count * rows), :]
@@ -277,23 +288,24 @@
         spread_fields[k, pl.ds(own_f, size0), :] = field_ref[k + 1]
     for mix in (mix_a, mix_b, mix_c, mix_d, mix_e, mix_f):
         mix[:, pl.ds(rows, 8), :] = jnp.zeros((mix.shape[0], 8, LANES), F32)
-    for pair in c_halos:
-        arrived(pair)
-
-    @pl.loop(0, width + 1)
-    def _(turn):
-        lane = lax.broadcasted_iota(jnp.int32, (rows, LANES), 1)
-        line_at = lax.broadcasted_iota(jnp.int32, (rows, LANES), 0)
-        base = pl.multiple_of(turn * rows, 8)
-        for k in range(KL + 1):
-            ref = c0 if k == 0 else spread_fields.at[k - 1]
-            shift = own0 - rows if k == 0 else PAD
-            here = ref[pl.ds(shift + base, rows), :]
-            face_x[k, pl.ds(base, rows), :] = 0.5 * (here + ref[pl.ds(shift + base + rows, rows), :])
-            face_y[k, pl.ds(base, rows), :] = jnp.where(
-                line_at < rows - 1, 0.5 * (here + ref[pl.ds(shift + base + 1, rows), :]), 0.0)
-            face_z[k, pl.ds(base, rows), :] = jnp.where(
-                lane < LANES - 1, 0.5 * (here + pltpu.roll(here, LANES - 1, 1)), 0.0)
+    def all_faces():
+        for pair in c_halos:
+            arrived(pair)
+
+        @pl.loop(0, width + 1)
+        def _(turn):
+            lane = lax.broadcasted_iota(jnp.int32, (rows, LANES), 1)
+            line_at = lax.broadcasted_iota(jnp.int32, (rows, LANES), 0)
+            base = pl.multiple_of(turn * rows, 8)
+            for k in range(KL + 1):
+                ref = c0 if k == 0 else spread_fields.at[k - 1]
+                shift = own0 - rows if k == 0 else PAD
+                here = ref[pl.ds(shift + base, rows), :]
+                face_x[k, pl.ds(base, rows), :] = 0.5 * (here + ref[pl.ds(shift + base + rows, rows), :])
+                face_y[k, pl.ds(base, rows), :] = jnp.where(
+                    line_at < rows - 1, 0.5 * (here + ref[pl.ds(shift + base + 1, rows), :]), 0.0)
+                face_z[k, pl.ds(base, rows), :] = jnp.where(
+                    lane < LANES - 1, 0.5 * (here + pltpu.roll(here, LANES - 1, 1)), 0.0)
 
     def source_of(x):
         if x < 0:
@@ -368,127 +380,153 @@
     def partner_step(now, later, hold, x, emits=True):
         advance(modes, KL, now, later, hold, x, emit_partner(x) if emits else None)
 
-    last = width - 1
+    merge = pairing()
+    spread = spreading()
+    own1 = PAD + 5 * r1
+    size1 = n1 * r1
+    own2 = PAD + 6 * r2
+    size2 = n2 * r2
+    columns = grid // 8
+    all3 = columns * r3
+
+    def gather_small(value, dest, turn):
+        slots[turn, row_at, pl.ds(0, r3), :] = value
+        copies = []
+        for q in range(1, ROW):
+            copy = start_copy(slots.at[turn, row_at], slots.at[turn, row_at], row_peer(q))
+            sends.append((copy, None))
+            copies.append((copy, None))
+
+        def second():
+            for pair in copies:
+                arrived(pair)
+            first = pl.multiple_of(PAD + col_at * (ROW * r3), 8)
+            for n in range(0, ROW, 2):
+                dest[pl.ds(first + n * r3, 2 * r3), :] = jnp.concatenate(
+                    [slots[turn, n, pl.ds(0, r3), :], slots[turn, n + 1, pl.ds(0, r3), :]], axis=0)
+            at = pl.ds(first, ROW * r3)
+            more = []
+            for q in range(1, cols):
+                copy = start_copy(dest.at[at], dest.at[at], col_peer(q))
+                sends.append((copy, None))
+                more.append((copy, None))
+            return more
+
+        return second
+
+    def coarse_coefficients():
+        part = pair_xy(c0, own0, width, rows, temp)
+        c1[pl.ds(own1, size1), :] = restrict_pair(part, part, merge)
+        found = [
+            to_neighbour(c1.at[pl.ds(own1, size1)], c1.at[pl.ds(own1 - size1, size1)], 1),
+            to_neighbour(c1.at[pl.ds(own1, size1)], c1.at[pl.ds(own1 + size1, size1)], -1),
+            to_neighbour(c1.at[pl.ds(own1 + size1 - r1, r1)], c1.at[pl.ds(own1 - size1 - r1, r1)], 2),
+            to_neighbour(c1.at[pl.ds(own1, r1)], c1.at[pl.ds(own1 + 2 * size1, r1)], -2),
+        ]
+        part = pair_xy(c1, own1, n1, r1, temp)
+        c2[pl.ds(own2, size2), :] = restrict_pair(part, part, merge)
+        for delta in NEAR:
+            found.append(to_neighbour(c2.at[pl.ds(own2, size2)], c2.at[pl.ds(own2 - delta * size2, size2)], delta))
+        part = pair_xy(c2, own2, n2, r2, temp)
+        return found, gather_small(restrict_pair(part, part, merge), c3, 0)
+
+    def column_sums(values):
+        gather = jnp.where(
+            lax.broadcasted_iota(jnp.int32, (columns, all3), 1) // r3
+            == lax.broadcasted_iota(jnp.int32, (columns, all3), 0), 1.0, 0.0)
+        within = jnp.where(
+            lax.broadcasted_iota(jnp.int32, (LANES, LANES), 1) // (LANES // 8)
+            == lax.broadcasted_iota(jnp.int32, (LANES, LANES), 0) // (LANES // 8), 1.0, 0.0)
+        return jnp.dot(
+            jnp.dot(gather, values, precision=lax.Precision.HIGHEST, preferred_element_type=F32),
+            within, precision=lax.Precision.HIGHEST, preferred_element_type=F32)
+
+    def line_factors():
+        diag3 = i3[pl.ds(PAD, all3), :]
+        line[0] = column_sums(g3[1, pl.ds(PAD, all3), :] * diag3)
+        line[2] = column_sums(g3[0, pl.ds(PAD, all3), :] * diag3)
+        ratio = None
+        for x in range(columns):
+            low, high = line[0, pl.ds(x, 1), :], line[2, pl.ds(x, 1), :]
+            den = low + high
+            if ratio is not None:
+                den = den - low * ratio
+            inv = 1.0 / den
+            ratio = high * inv
+            line[0, pl.ds(x, 1), :] = low * inv
+            line[1, pl.ds(x, 1), :] = inv
+            line[2, pl.ds(x, 1), :] = ratio
+
+    all_faces()
     pass_on(0)
     send_own(2)
+    coarse_halos, coarse_second = coarse_coefficients()
     pass_on(1)
     send_own(3)
     complete(0)
     low = to_neighbour(q0, rim_low, 1)
+    for ref in (s3, a3, d3):
+        zero_all(ref)
+    pass_on(2)
+    send_own(4)
     complete(1)
     high = to_neighbour(q1, rim_high, -1)
-    pass_on(2)
-    send_own(4)
+    for ref in (s2, a2, d2, s1, a1, d1):
+        zero_all(ref)
+    pass_on(3)
+    send_own(5)
     complete(2)
     arrived(low)
     fill(modes, KL, mix_a, -1)
     partner_step(mix_a, mix_b, hold_a, -1, False)
     partner_step(mix_b, mix_a, hold_a, 0)
     send_partner(0)
-    pass_on(3)
+    pass_on(4)
+    send_own(6)
+    c3_more = coarse_second()
+    complete(3)
     partner_step(mix_a, mix_b, hold_a, 1)
     send_partner(1)
-    complete(3)
+    pass_on(5)
+    send_own(7)
+    for pair in coarse_halos:
+        arrived(pair)
+    level_faces(c1, g1, w1, i1, PAD + r1, (n1 + 8) * r1, 16, r1, LANES // 2, 0.25, me * n1 - 5, grid // 2)
+    level_faces(c2, g2, w2, i2, PAD + r2, (n2 + 10) * r2, 16, r2, LANES // 4, 0.0625, me * n2 - 6, grid // 4)
+    pass_on(6)
+    complete(4)
+    complete(5)
     arrived(high)
     fill(modes, KL, mix_c, 5)
     partner_step(mix_c, mix_d, hold_b, 5, False)
     partner_step(mix_d, mix_c, hold_b, 6)
     send_partner(6)
-    pass_on(4)
+    pass_on(7)
     partner_step(mix_c, mix_d, hold_b, 7)
     send_partner(7)
-    complete(4)
+    complete(6)
     partner_step(mix_b, mix_a, hold_a, 2)
     send_partner(2)
+    complete(7)
     partner_step(mix_a, mix_b, hold_a, 3)
     partner_step(mix_b, mix_a, hold_a, 4)
     partner_step(mix_a, mix_b, hold_a, 5)
     send_partner(5)
-    send_partner(3)
-    send_partner(4)
     fill(0, KL + 1, mix_e, -1)
     now, later = mix_e, mix_f
     for x in range(-1, width):
         advance(0, KL + 1, now, later, hold_c, x, emit_own(x) if x >= 0 else None)
         now, later = later, now
-    for ref in (s0, a0, d0, s1, a1, d1, s2, a2, d2, s3, a3, d3):
+        if x == 1:
+            send_partner(3)
+            send_partner(4)
+    level_faces(c0, g0, w0, i0, PAD + rows, (width + 6) * rows, 16, rows, LANES, 1.0, me * width - 4, grid)
+    for pair in c3_more:
+        arrived(pair)
+    level_faces(c3, g3, w3, i3, PAD, all3, 32, r3, LANES // 8, 0.015625, 0, grid // 8)
+    line_factors()
+    for ref in (s0, a0, d0):
         zero_all(ref)
-    for ref in (c2, c3):
-        ref[pl.ds(0, PAD), :] = jnp.zeros((PAD, LANES), F32)
-        ref[pl.ds(ref.shape[0] - PAD, PAD), :] = jnp.zeros((PAD, LANES), F32)
-
-    merge = pairing()
-    spread = spreading()
-
-    own1 = PAD + 5 * r1
-    size1 = n1 * r1
-    part = pair_xy(c0, own0, width, rows, temp)
-    c1[pl.ds(own1, size1), :] = restrict_pair(part, part, merge)
-    c1_halos = [
-        to_neighbour(c1.at[pl.ds(own1, size1)], c1.at[pl.ds(own1 - size1, size1)], 1),
-        to_neighbour(c1.at[pl.ds(own1, size1)], c1.at[pl.ds(own1 + size1, size1)], -1),
-        to_neighbour(c1.at[pl.ds(own1 + size1 - r1, r1)], c1.at[pl.ds(own1 - size1 - r1, r1)], 2),
-        to_neighbour(c1.at[pl.ds(own1, r1)], c1.at[pl.ds(own1 + 2 * size1, r1)], -2),
-    ]
-    size2 = n2 * r2
-    own2 = pl.multiple_of(PAD + me * size2, 8)
-    group2 = pl.multiple_of(PAD + col_at * (ROW * size2), 8)
-    part = pair_xy(c1, own1, n1, r1, temp)
-    c2[pl.ds(own2, size2), :] = restrict_pair(part, part, merge)
-    c2_row = []
-    for q in range(1, ROW):
-        copy = start_copy(c2.at[pl.ds(own2, size2)], c2.at[pl.ds(own2, size2)], row_peer(q))
-        sends.append((copy, None))
-        c2_row.append((copy, None))
-
-    level_faces(c0, g0, w0, i0, PAD + rows, (width + 6) * rows, 16, rows, LANES, 1.0, me * width - 4, grid)
-
-    for pair in c2_row:
-        arrived(pair)
-    c2_col = []
-    for q in range(1, cols):
-        at = pl.ds(group2, ROW * size2)
-        copy = start_copy(c2.at[at], c2.at[at], col_peer(q))
-        sends.append((copy, None))
-        c2_col.append((copy, None))
-    for pair in c1_halos:
-        arrived(pair)
-    level_faces(c1, g1, w1, i1, PAD + r1, (n1 + 8) * r1, 16, r1, LANES // 2, 0.25, me * n1 - 5, grid // 2)
-    for pair in c2_col:
-        arrived(pair)
-    all2 = blocks * size2
-    level_faces(c2, g2, w2, i2, PAD, all2, 32, r2, LANES // 4, 0.0625, 0, grid // 4)
-    part = pair_xy(c2, PAD, blocks * n2, r2, temp)
-    all3 = all2 // 4
-    c3[pl.ds(PAD, all3), :] = restrict_pair(part, part, merge)
-    level_faces(c3, g3, w3, i3, PAD, all3, 32, r3, LANES // 8, 0.015625, 0, grid // 8)
-    columns = grid // 8
-    gather = jnp.where(
-        lax.broadcasted_iota(jnp.int32, (columns, all3), 1) // r3
-        == lax.broadcasted_iota(jnp.int32, (columns, all3), 0), 1.0, 0.0)
-    within = jnp.where(
-        lax.broadcasted_iota(jnp.int32, (LANES, LANES), 1) // (LANES // 8)
-        == lax.broadcasted_iota(jnp.int32, (LANES, LANES), 0) // (LANES // 8), 1.0, 0.0)
-
-    def column_sums(values):
-        return jnp.dot(
-            jnp.dot(gather, values, precision=lax.Precision.HIGHEST, preferred_element_type=F32),
-            within, precision=lax.Precision.HIGHEST, preferred_element_type=F32)
-
-    diag3 = i3[pl.ds(PAD, all3), :]
-    line[0] = column_sums(g3[1, pl.ds(PAD, all3), :] * diag3)
-    line[2] = column_sums(g3[0, pl.ds(PAD, all3), :] * diag3)
-    ratio = None
-    for x in range(columns):
-        low, high = line[0, pl.ds(x, 1), :], line[2, pl.ds(x, 1), :]
-        den = low + high
-        if ratio is not None:
-            den = den - low * ratio
-        inv = 1.0 / den
-        ratio = high * inv
-        line[0, pl.ds(x, 1), :] = low * inv
-        line[1, pl.ds(x, 1), :] = inv
-        line[2, pl.ds(x, 1), :] = ratio
 
     def receive(x):
         to_partner[x].wait_recv()
@@ -507,12 +545,15 @@
     halos.append(to_neighbour(b0.at[pl.ds(0, modes), pl.ds(own0 + size0 - 3 * rows, 3 * rows)], b0.at[pl.ds(0, modes), pl.ds(own0 - 3 * rows, 3 * rows)], 1))
     for x in (3, 4):
         receive(x)
+    first_sweep(s0, b0, w0, modes, own0, size0, 16)
+    sweep(a0, s0, s0, g0, modes, own0 + rows, size0 - 2 * rows, 16, rows)
     for pair in halos:
         arrived(pair)
-    first_sweep(s0, b0, w0, modes, PAD + rows, (width + 6) * rows, 16)
-    sweep(a0, s0, s0, g0, modes, PAD + 2 * rows, (width + 4) * rows, 16, rows)
+    for at in (own0 - 3 * rows, own0 + size0):
+        first_sweep(s0, b0, w0, modes, at, 3 * rows, 16)
+    for at in (own0 - 2 * rows, own0 + size0 - rows):
+        sweep(a0, s0, s0, g0, modes, at, 3 * rows, 16, rows)
     sweep(d0, a0, s0, g0, modes, own0, size0, 16, rows, inverse=i0)
-
     pairs1 = b1.shape[0]
     for p in range(pairs1):
         left = pair_xy(d0.at[2 * p], own0, width, rows, temp)
@@ -532,36 +573,26 @@
         left = pair_xy(d1.at[2 * p], own1, n1, r1, temp)
         right = pair_xy(d1.at[2 * p + 1], own1, n1, r1, temp)
         b2[p, pl.ds(own2, size2), :] = restrict_pair(left, right, merge)
-    row_copies = []
-    for q in range(1, ROW):
-        at = pl.ds(own2, size2)
-        copy = start_copy(b2.at[:, at], b2.at[:, at], row_peer(q))
-        sends.append((copy, None))
-        row_copies.append((copy, None))
-    for pair in row_copies:
+    b2_halos = []
+    for delta in NEAR:
+        b2_halos.append(to_neighbour(b2.at[:, pl.ds(own2, size2)], b2.at[:, pl.ds(own2 - delta * size2, size2)], delta))
+    for pair in b2_halos:
         arrived(pair)
-    col_copies = []
-    for q in range(1, cols):
-        at = pl.ds(group2, ROW * size2)
-        copy = start_copy(b2.at[:, at], b2.at[:, at], col_peer(q))
-        sends.append((copy, None))
-        col_copies.append((copy, None))
-    for pair in col_copies:
+    first_sweep(s2, b2, w2, pairs2, PAD + r2, (n2 + 10) * r2, 16)
+    sweep(a2, s2, s2, g2, pairs2, PAD + 2 * r2, (n2 + 8) * r2, 16, r2)
+    sweep(d2, a2, s2, g2, pairs2, own2, size2, 16, r2, inverse=i2)
+    left = pair_xy(d2.at[0], own2, n2, r2, temp)
+    right = pair_xy(d2.at[1], own2, n2, r2, temp)
+    second = gather_small(restrict_pair(left, right, merge), b3.at[0], 1)
+    for pair in second():
         arrived(pair)
-
-    first_sweep(s2, b2, w2, pairs2, PAD, all2, 32)
-    sweep(a2, s2, s2, g2, pairs2, PAD, all2, 32, r2)
-    sweep(d2, a2, s2, g2, pairs2, PAD, all2, 32, r2, inverse=i2)
-    left = pair_xy(d2.at[0], PAD, blocks * n2, r2, temp)
-    right = pair_xy(d2.at[1], PAD, blocks * n2, r2, temp)
-    b3[0, pl.ds(PAD, all3), :] = restrict_pair(left, right, merge)
     first_sweep(s3, b3, w3, 1, PAD, all3, 32)
     now, other = s3, a3
     for turn in range(COARSE - 1):
         sweep(other, now, s3, g3, 1, PAD, all3, 32, r3)
         now, other = (a3, d3) if now is s3 else (other, now)
-    sweep(b3, now, s3, g3, 1, PAD, all3, 32, r3, inverse=i3)
-    sums[...] = column_sums(b3[0, pl.ds(PAD, all3), :])
+    sweep(other, now, s3, g3, 1, PAD, all3, 32, r3, inverse=i3)
+    sums[...] = column_sums(other[0, pl.ds(PAD, all3), :])
     carried = None
     for x in range(columns):
         value = sums[pl.ds(x, 1), :] * line[1, pl.ds(x, 1), :]
@@ -577,23 +608,18 @@
         carried = value
         at = pl.ds(PAD + x * r3, r3)
         now[0, at, :] = now[0, at, :] + jnp.broadcast_to(value, (r3, LANES))
-    prolong(a2, pairs2, PAD, now, PAD, columns, r3, spread, temp)
-    sweep(d2, a2, s2, g2, pairs2, PAD, all2, 32, r2)
-    sweep(a2, d2, s2, g2, pairs2, PAD, all2, 32, r2)
-    window = pl.multiple_of(PAD + me * size2 - 2 * r2, 8)
-    prolong(a1, pairs1, PAD + r1, a2, window, n2 + 4, r2, spread, temp)
+    for x in range(5):
+        small[pl.ds(x * r3, r3), :] = now[0, pl.ds(PAD + (me + x - 2) * r3, r3), :]
+    prolong(a2, pairs2, PAD + 2 * r2, lambda p: small[pl.ds(0, 5 * r3), :], 5, r3, spread, temp)
+    sweep(d2, a2, s2, g2, pairs2, PAD + 3 * r2, (n2 + 6) * r2, 16, r2)
+    sweep(a2, d2, s2, g2, pairs2, PAD + 4 * r2, (n2 + 4) * r2, 16, r2)
+    prolong(a1, pairs1, PAD + r1, lambda p: a2[p, pl.ds(PAD + 4 * r2, (n2 + 4) * r2), :], n2 + 4, r2, spread, temp)
     sweep(d1, a1, s1, g1, pairs1, PAD + 3 * r1, (n1 + 4) * r1, 16, r1)
     sweep(a1, d1, s1, g1, pairs1, PAD + 4 * r1, (n1 + 2) * r1, 16, r1)
-    prolong(a0, modes, PAD + 2 * rows, a1, PAD + 4 * r1, n1 + 2, r1, spread, temp)
+    prolong(a0, modes, PAD + 2 * rows, lambda p: a1[p, pl.ds(PAD + 4 * r1, (n1 + 2) * r1), :], n1 + 2, r1, spread, temp)
     sweep(d0, a0, s0, g0, modes, PAD + 3 * rows, (width + 2) * rows, 16, rows)
     sweep(a0, d0, s0, g0, modes, own0, size0, 16, rows)
-    for m in range(modes):
-        out_ref[m] = a0[m, pl.ds(own0, size0), :]
-    for copy, exists in sends:
-        if exists is None:
-            copy.wait_send()
-        else:
-            pl.when(exists)(copy.wait_send)
+    finish()
 
 
 def coupling_places(coupling_list, mode, modes):
@@ -624,20 +650,20 @@
     grid = width * blocks
     n0 = (width + 8) * rows + 2 * PAD
     n1 = (width // 2 + 10) * r1 + 2 * PAD
-    n2 = grid // 4 * r2 + 2 * PAD
+    n2 = (width // 4 + 12) * r2 + 2 * PAD
     n3 = grid // 8 * r3 + 2 * PAD
     scratch = []
     for size, count in ((n0, even), (n1, even // 2), (n2, even // 4), (n3, 1)):
         scratch += [pltpu.VMEM((size, LANES), F32)] * 3
         scratch += [pltpu.VMEM((6, size, LANES), F32)]
         scratch += [pltpu.VMEM((count, size, LANES), F32)] * 4
-    cycle_copies = 4 + 4 + 2 + 2 * (ROW - 1 + blocks // ROW - 1)
-    copies = cycle_copies + 4 * len(CHUNKS) + 4 + width
     held = RING * modes
     scratch += [
-        pltpu.VMEM((grid // 4 * r2, LANES), F32),
+        pltpu.VMEM((512, LANES), F32),
         pltpu.VMEM((3, grid // 8, LANES), F32),
         pltpu.VMEM((grid // 8, LANES), F32),
+        pltpu.VMEM((24, LANES), F32),
+        pltpu.VMEM((2, ROW, 8, LANES), F32),
     ]
     scratch += [pltpu.VMEM((held, count * rows, LANES), F32) for _, count in CHUNKS]
     scratch += [pltpu.VMEM((held, rows, LANES), F32)] * 2
@@ -647,7 +673,7 @@
     scratch += [pltpu.VMEM((modes * (KL + 1), rows + 8, LANES), F32)] * 2
     scratch += [pltpu.VMEM((modes, rows, LANES), F32)] * 3
     scratch += [pltpu.VMEM((width, modes, rows, LANES), F32)] * 2
-    scratch += [pltpu.SemaphoreType.DMA((copies,))] * 2
+    scratch += [pltpu.SemaphoreType.DMA((COPIES,))] * 2
     geometry = (modes, width, rows, blocks)
     places, shares = coupling_places(coupling_list, lax.axis_index("mode"), modes)
     shape = jax.ShapeDtypeStruct((modes, plane, depth), F32)

time: 141 us -> 117 us (0.83)
  Pallas kernels: 135 us -> 109 us
    pallas_call x1, Pallas kernels: 135 us -> 109 us  [local(): pl.pallas_call(lambda *refs: cycle_kernel(geometry, *refs), out_shape=(sh...]
where the time goes in v3:
time: 117 us; the launch traced here: 115 us
  Pallas kernels  109 us (93%)
  local copies, waits for them, and re-layouts  3.88 us (3%)
  other arithmetic  1.59 us (1%)
    pallas_call x1, Pallas kernels, local(): pl.pallas_call(lambda *refs: cycle_kernel(geometry, *refs), out_shape=(sh...  109 us
    unnamed x6, local copies, waits for them, and re-layouts  3.79 us

profile of v3, /device:TPU:32, one launch (start us, length us, event | category | flops | bytes accessed | tf_op | source)
XLA Modules:
  0.0 115.4 jit_solution(4546238469323649599)
XLA Ops:
  0.7 0.0 copy-start.1
  0.7 0.1 add_multiply_fusion
  0.7 0.6 copy-done.1
  1.4 0.1 broadcast_add_fusion
  1.5 0.1 add.92
  1.6 0.2 select_reduce_fusion.1
  1.8 0.6 and_select_fusion.3.refs_0_
  2.4 0.6 fusion.3.refs_1_
  3.0 109.2 %coupled_cycle.1 = (f32[7,256,128]{2,1,0:T(8,128)}, f32[7,256,128]{2,1,0:T(8,128)}) custom-call(s32[2,70]{1,0:T(2,128)} %and_select_fusion.3.refs_0_, f32[2,70]{1,0:T(2,128)} %fusion.3.refs_1_, f32[7,256,128]{2,1,0:T(8,128)} %bitcast.15, f32[7,256,128]{2,1,0:T(8,128)} %bitcast.16, f32[6,256,128]{2,1,0:T(8,128)} %bitcast.17), custom_call_target="tpu_custom_call" | custom-call | tf_op jit(solution)/shard_map/coupled_cycle/pallas_call | solution.py:680
  112.2 0.0 copy-start
  112.2 2.3 %copy.8 = f32[7,8,32,128]{3,2,1,0:T(8,128)} copy(f32[7,8,32,128]{3,2,1,0:T(8,128)} %bitcast.14) | data formatting | bytes 1835008
  114.5 0.0 copy-done
  114.5 0.9 copy.9
  (6 shorter events, 0.1 us)
Async XLA Ops:
  0.7 0.7 copy-start.1
  112.2 2.3 %copy-start = (f32[7,256,128]{2,1,0:T(8,128)S(1)}, f32[7,256,128]{2,1,0:T(8,128)}, u32[]{:S(2)}) copy-start(f32[7,256,128]{2,1,0:T(8,128)} %get-tuple-element.5) | copy-start | bytes 2752516

commit v4 on v3

--- a/solution.py
+++ b/solution.py
@@ -565,9 +565,9 @@
     ]
     for pair in b1_halos:
         arrived(pair)
-    first_sweep(s1, b1, w1, pairs1, PAD + r1, (n1 + 8) * r1, 16)
-    sweep(a1, s1, s1, g1, pairs1, PAD + 2 * r1, (n1 + 6) * r1, 16, r1)
-    sweep(d1, a1, s1, g1, pairs1, own1, size1, 16, r1, inverse=i1)
+    first_sweep(s1, b1, w1, pairs1, PAD + r1, (n1 + 8) * r1, 32)
+    sweep(a1, s1, s1, g1, pairs1, PAD + 2 * r1, (n1 + 6) * r1, 32, r1)
+    sweep(d1, a1, s1, g1, pairs1, own1, size1, 32, r1, inverse=i1)
     pairs2 = b2.shape[0]
     for p in range(pairs2):
         left = pair_xy(d1.at[2 * p], own1, n1, r1, temp)
@@ -578,20 +578,20 @@
         b2_halos.append(to_neighbour(b2.at[:, pl.ds(own2, size2)], b2.at[:, pl.ds(own2 - delta * size2, size2)], delta))
     for pair in b2_halos:
         arrived(pair)
-    first_sweep(s2, b2, w2, pairs2, PAD + r2, (n2 + 10) * r2, 16)
-    sweep(a2, s2, s2, g2, pairs2, PAD + 2 * r2, (n2 + 8) * r2, 16, r2)
+    first_sweep(s2, b2, w2, pairs2, PAD + r2, (n2 + 10) * r2, 48)
+    sweep(a2, s2, s2, g2, pairs2, PAD + 2 * r2, (n2 + 8) * r2, 40, r2)
     sweep(d2, a2, s2, g2, pairs2, own2, size2, 16, r2, inverse=i2)
     left = pair_xy(d2.at[0], own2, n2, r2, temp)
     right = pair_xy(d2.at[1], own2, n2, r2, temp)
     second = gather_small(restrict_pair(left, right, merge), b3.at[0], 1)
     for pair in second():
         arrived(pair)
-    first_sweep(s3, b3, w3, 1, PAD, all3, 32)
+    first_sweep(s3, b3, w3, 1, PAD, all3, all3)
     now, other = s3, a3
     for turn in range(COARSE - 1):
-        sweep(other, now, s3, g3, 1, PAD, all3, 32, r3)
+        sweep(other, now, s3, g3, 1, PAD, all3, all3, r3)
         now, other = (a3, d3) if now is s3 else (other, now)
-    sweep(other, now, s3, g3, 1, PAD, all3, 32, r3, inverse=i3)
+    sweep(other, now, s3, g3, 1, PAD, all3, all3, r3, inverse=i3)
     sums[...] = column_sums(other[0, pl.ds(PAD, all3), :])
     carried = None
     for x in range(columns):
@@ -611,11 +611,11 @@
     for x in range(5):
         small[pl.ds(x * r3, r3), :] = now[0, pl.ds(PAD + (me + x - 2) * r3, r3), :]
     prolong(a2, pairs2, PAD + 2 * r2, lambda p: small[pl.ds(0, 5 * r3), :], 5, r3, spread, temp)
-    sweep(d2, a2, s2, g2, pairs2, PAD + 3 * r2, (n2 + 6) * r2, 16, r2)
-    sweep(a2, d2, s2, g2, pairs2, PAD + 4 * r2, (n2 + 4) * r2, 16, r2)
+    sweep(d2, a2, s2, g2, pairs2, PAD + 3 * r2, (n2 + 6) * r2, 32, r2)
+    sweep(a2, d2, s2, g2, pairs2, PAD + 4 * r2, (n2 + 4) * r2, 48, r2)
     prolong(a1, pairs1, PAD + r1, lambda p: a2[p, pl.ds(PAD + 4 * r2, (n2 + 4) * r2), :], n2 + 4, r2, spread, temp)
-    sweep(d1, a1, s1, g1, pairs1, PAD + 3 * r1, (n1 + 4) * r1, 16, r1)
-    sweep(a1, d1, s1, g1, pairs1, PAD + 4 * r1, (n1 + 2) * r1, 16, r1)
+    sweep(d1, a1, s1, g1, pairs1, PAD + 3 * r1, (n1 + 4) * r1, 32, r1)
+    sweep(a1, d1, s1, g1, pairs1, PAD + 4 * r1, (n1 + 2) * r1, 32, r1)
     prolong(a0, modes, PAD + 2 * rows, lambda p: a1[p, pl.ds(PAD + 4 * r1, (n1 + 2) * r1), :], n1 + 2, r1, spread, temp)
     sweep(d0, a0, s0, g0, modes, PAD + 3 * rows, (width + 2) * rows, 16, rows)
     sweep(a0, d0, s0, g0, modes, own0, size0, 16, rows)

time: 117 us -> 114 us (0.974)
  Pallas kernels: 109 us -> 106 us
    pallas_call x1, Pallas kernels: 109 us -> 106 us  [local(): pl.pallas_call(lambda *refs: cycle_kernel(geometry, *refs), out_shape=(sh...]
where the time goes in v4:
time: 114 us; the launch traced here: 112 us
  Pallas kernels  106 us (93%)
  local copies, waits for them, and re-layouts  3.88 us (3%)
  other arithmetic  1.59 us (1%)
    pallas_call x1, Pallas kernels, local(): pl.pallas_call(lambda *refs: cycle_kernel(geometry, *refs), out_shape=(sh...  106 us
    unnamed x6, local copies, waits for them, and re-layouts  3.79 us

profile of v4, /device:TPU:32, one launch (start us, length us, event | category | flops | bytes accessed | tf_op | source)
XLA Modules:
  0.0 112.3 jit_solution(4171520884354670934)
XLA Ops:
  0.7 0.0 copy-start.1
  0.7 0.1 add_multiply_fusion
  0.7 0.6 copy-done.1
  1.4 0.1 broadcast_add_fusion
  1.5 0.1 add.92
  1.6 0.2 select_reduce_fusion.1
  1.8 0.6 and_select_fusion.3.refs_0_
  2.4 0.6 fusion.3.refs_1_
  3.0 106.1 %coupled_cycle.1 = (f32[7,256,128]{2,1,0:T(8,128)}, f32[7,256,128]{2,1,0:T(8,128)}) custom-call(s32[2,70]{1,0:T(2,128)} %and_select_fusion.3.refs_0_, f32[2,70]{1,0:T(2,128)} %fusion.3.refs_1_, f32[7,256,128]{2,1,0:T(8,128)} %bitcast.15, f32[7,256,128]{2,1,0:T(8,128)} %bitcast.16, f32[6,256,128]{2,1,0:T(8,128)} %bitcast.17), custom_call_target="tpu_custom_call" | custom-call | tf_op jit(solution)/shard_map/coupled_cycle/pallas_call | solution.py:680
  109.1 0.0 copy-start
  109.1 2.3 %copy.8 = f32[7,8,32,128]{3,2,1,0:T(8,128)} copy(f32[7,8,32,128]{3,2,1,0:T(8,128)} %bitcast.14) | data formatting | bytes 1835008
  111.3 0.0 copy-done
  111.3 0.9 copy.9
  (6 shorter events, 0.1 us)
Async XLA Ops:
  0.7 0.7 copy-start.1
  109.1 2.3 %copy-start = (f32[7,256,128]{2,1,0:T(8,128)S(1)}, f32[7,256,128]{2,1,0:T(8,128)}, u32[]{:S(2)}) copy-start(f32[7,256,128]{2,1,0:T(8,128)} %get-tuple-element.5) | copy-start | bytes 2752516

commit v5 on v4

--- a/solution.py
+++ b/solution.py
@@ -545,15 +545,15 @@
     halos.append(to_neighbour(b0.at[pl.ds(0, modes), pl.ds(own0 + size0 - 3 * rows, 3 * rows)], b0.at[pl.ds(0, modes), pl.ds(own0 - 3 * rows, 3 * rows)], 1))
     for x in (3, 4):
         receive(x)
-    first_sweep(s0, b0, w0, modes, own0, size0, 16)
-    sweep(a0, s0, s0, g0, modes, own0 + rows, size0 - 2 * rows, 16, rows)
+    first_sweep(s0, b0, w0, modes, own0, size0, 32)
+    sweep(a0, s0, s0, g0, modes, own0 + rows, size0 - 2 * rows, 32, rows)
     for pair in halos:
         arrived(pair)
     for at in (own0 - 3 * rows, own0 + size0):
-        first_sweep(s0, b0, w0, modes, at, 3 * rows, 16)
+        first_sweep(s0, b0, w0, modes, at, 3 * rows, 32)
     for at in (own0 - 2 * rows, own0 + size0 - rows):
-        sweep(a0, s0, s0, g0, modes, at, 3 * rows, 16, rows)
-    sweep(d0, a0, s0, g0, modes, own0, size0, 16, rows, inverse=i0)
+        sweep(a0, s0, s0, g0, modes, at, 3 * rows, 32, rows)
+    sweep(d0, a0, s0, g0, modes, own0, size0, 32, rows, inverse=i0)
     pairs1 = b1.shape[0]
     for p in range(pairs1):
         left = pair_xy(d0.at[2 * p], own0, width, rows, temp)
@@ -617,8 +617,8 @@
     sweep(d1, a1, s1, g1, pairs1, PAD + 3 * r1, (n1 + 4) * r1, 32, r1)
     sweep(a1, d1, s1, g1, pairs1, PAD + 4 * r1, (n1 + 2) * r1, 32, r1)
     prolong(a0, modes, PAD + 2 * rows, lambda p: a1[p, pl.ds(PAD + 4 * r1, (n1 + 2) * r1), :], n1 + 2, r1, spread, temp)
-    sweep(d0, a0, s0, g0, modes, PAD + 3 * rows, (width + 2) * rows, 16, rows)
-    sweep(a0, d0, s0, g0, modes, own0, size0, 16, rows)
+    sweep(d0, a0, s0, g0, modes, PAD + 3 * rows, (width + 2) * rows, 32, rows)
+    sweep(a0, d0, s0, g0, modes, own0, size0, 32, rows)
     finish()
 
 

time: 114 us -> 112 us (0.982)
  Pallas kernels: 106 us -> 104 us
    pallas_call x1, Pallas kernels: 106 us -> 104 us  [local(): pl.pallas_call(lambda *refs: cycle_kernel(geometry, *refs), out_shape=(sh...]
where the time goes in v5:
time: 112 us; the launch traced here: 110 us
  Pallas kernels  104 us (93%)
  local copies, waits for them, and re-layouts  3.88 us (3%)
  other arithmetic  1.59 us (1%)
    pallas_call x1, Pallas kernels, local(): pl.pallas_call(lambda *refs: cycle_kernel(geometry, *refs), out_shape=(sh...  104 us
    unnamed x6, local copies, waits for them, and re-layouts  3.79 us

profile of v5, /device:TPU:32, one launch (start us, length us, event | category | flops | bytes accessed | tf_op | source)
XLA Modules:
  0.0 109.7 jit_solution(17403216810885150594)
XLA Ops:
  0.7 0.0 copy-start.1
  0.7 0.1 add_multiply_fusion
  0.7 0.6 copy-done.1
  1.4 0.1 broadcast_add_fusion
  1.5 0.1 add.92
  1.6 0.2 select_reduce_fusion.1
  1.8 0.6 and_select_fusion.3.refs_0_
  2.4 0.6 fusion.3.refs_1_
  3.0 103.6 %coupled_cycle.1 = (f32[7,256,128]{2,1,0:T(8,128)}, f32[7,256,128]{2,1,0:T(8,128)}) custom-call(s32[2,70]{1,0:T(2,128)} %and_select_fusion.3.refs_0_, f32[2,70]{1,0:T(2,128)} %fusion.3.refs_1_, f32[7,256,128]{2,1,0:T(8,128)} %bitcast.15, f32[7,256,128]{2,1,0:T(8,128)} %bitcast.16, f32[6,256,128]{2,1,0:T(8,128)} %bitcast.17), custom_call_target="tpu_custom_call" | custom-call | tf_op jit(solution)/shard_map/coupled_cycle/pallas_call | solution.py:680
  106.5 0.0 copy-start
  106.5 2.3 %copy.8 = f32[7,8,32,128]{3,2,1,0:T(8,128)} copy(f32[7,8,32,128]{3,2,1,0:T(8,128)} %bitcast.14) | data formatting | bytes 1835008
  108.8 0.0 copy-done
  108.8 0.9 copy.9
  (6 shorter events, 0.1 us)
Async XLA Ops:
  0.7 0.7 copy-start.1
  106.5 2.3 %copy-start = (f32[7,256,128]{2,1,0:T(8,128)S(1)}, f32[7,256,128]{2,1,0:T(8,128)}, u32[]{:S(2)}) copy-start(f32[7,256,128]{2,1,0:T(8,128)} %get-tuple-element.5) | copy-start | bytes 2752516

commit v6 on v5

--- a/solution.py
+++ b/solution.py
@@ -546,14 +546,14 @@
     for x in (3, 4):
         receive(x)
     first_sweep(s0, b0, w0, modes, own0, size0, 32)
-    sweep(a0, s0, s0, g0, modes, own0 + rows, size0 - 2 * rows, 32, rows)
+    sweep(a0, s0, s0, g0, modes, own0 + rows, size0 - 2 * rows, 64, rows)
     for pair in halos:
         arrived(pair)
     for at in (own0 - 3 * rows, own0 + size0):
         first_sweep(s0, b0, w0, modes, at, 3 * rows, 32)
     for at in (own0 - 2 * rows, own0 + size0 - rows):
         sweep(a0, s0, s0, g0, modes, at, 3 * rows, 32, rows)
-    sweep(d0, a0, s0, g0, modes, own0, size0, 32, rows, inverse=i0)
+    sweep(d0, a0, s0, g0, modes, own0, size0, 64, rows, inverse=i0)
     pairs1 = b1.shape[0]
     for p in range(pairs1):
         left = pair_xy(d0.at[2 * p], own0, width, rows, temp)
@@ -566,8 +566,8 @@
     for pair in b1_halos:
         arrived(pair)
     first_sweep(s1, b1, w1, pairs1, PAD + r1, (n1 + 8) * r1, 32)
-    sweep(a1, s1, s1, g1, pairs1, PAD + 2 * r1, (n1 + 6) * r1, 32, r1)
-    sweep(d1, a1, s1, g1, pairs1, own1, size1, 32, r1, inverse=i1)
+    sweep(a1, s1, s1, g1, pairs1, PAD + 2 * r1, (n1 + 6) * r1, 80, r1)
+    sweep(d1, a1, s1, g1, pairs1, own1, size1, 64, r1, inverse=i1)
     pairs2 = b2.shape[0]
     for p in range(pairs2):
         left = pair_xy(d1.at[2 * p], own1, n1, r1, temp)
@@ -614,11 +614,11 @@
     sweep(d2, a2, s2, g2, pairs2, PAD + 3 * r2, (n2 + 6) * r2, 32, r2)
     sweep(a2, d2, s2, g2, pairs2, PAD + 4 * r2, (n2 + 4) * r2, 48, r2)
     prolong(a1, pairs1, PAD + r1, lambda p: a2[p, pl.ds(PAD + 4 * r2, (n2 + 4) * r2), :], n2 + 4, r2, spread, temp)
-    sweep(d1, a1, s1, g1, pairs1, PAD + 3 * r1, (n1 + 4) * r1, 32, r1)
-    sweep(a1, d1, s1, g1, pairs1, PAD + 4 * r1, (n1 + 2) * r1, 32, r1)
+    sweep(d1, a1, s1, g1, pairs1, PAD + 3 * r1, (n1 + 4) * r1, 64, r1)
+    sweep(a1, d1, s1, g1, pairs1, PAD + 4 * r1, (n1 + 2) * r1, 48, r1)
     prolong(a0, modes, PAD + 2 * rows, lambda p: a1[p, pl.ds(PAD + 4 * r1, (n1 + 2) * r1), :], n1 + 2, r1, spread, temp)
-    sweep(d0, a0, s0, g0, modes, PAD + 3 * rows, (width + 2) * rows, 32, rows)
-    sweep(a0, d0, s0, g0, modes, own0, size0, 32, rows)
+    sweep(d0, a0, s0, g0, modes, PAD + 3 * rows, (width + 2) * rows, 64, rows)
+    sweep(a0, d0, s0, g0, modes, own0, size0, 64, rows)
     finish()
 
 

time: 112 us -> 110 us (0.982)
  Pallas kernels: 104 us -> 102 us
    pallas_call x1, Pallas kernels: 104 us -> 102 us  [local(): pl.pallas_call(lambda *refs: cycle_kernel(geometry, *refs), out_shape=(sh...]
where the time goes in v6:
time: 110 us; the launch traced here: 108 us
  Pallas kernels  102 us (93%)
  local copies, waits for them, and re-layouts  3.88 us (4%)
  other arithmetic  1.59 us (1%)
    pallas_call x1, Pallas kernels, local(): pl.pallas_call(lambda *refs: cycle_kernel(geometry, *refs), out_shape=(sh...  102 us
    unnamed x6, local copies, waits for them, and re-layouts  3.79 us

profile of v6, /device:TPU:32, one launch (start us, length us, event | category | flops | bytes accessed | tf_op | source)
XLA Modules:
  0.0 108.4 jit_solution(4458444175793176971)
XLA Ops:
  0.7 0.0 copy-start.1
  0.7 0.1 add_multiply_fusion
  0.7 0.6 copy-done.1
  1.4 0.1 broadcast_add_fusion
  1.5 0.1 add.92
  1.6 0.2 select_reduce_fusion.1
  1.8 0.6 and_select_fusion.3.refs_0_
  2.4 0.6 fusion.3.refs_1_
  3.0 102.2 %coupled_cycle.1 = (f32[7,256,128]{2,1,0:T(8,128)}, f32[7,256,128]{2,1,0:T(8,128)}) custom-call(s32[2,70]{1,0:T(2,128)} %and_select_fusion.3.refs_0_, f32[2,70]{1,0:T(2,128)} %fusion.3.refs_1_, f32[7,256,128]{2,1,0:T(8,128)} %bitcast.15, f32[7,256,128]{2,1,0:T(8,128)} %bitcast.16, f32[6,256,128]{2,1,0:T(8,128)} %bitcast.17), custom_call_target="tpu_custom_call" | custom-call | tf_op jit(solution)/shard_map/coupled_cycle/pallas_call | solution.py:680
  105.2 0.0 copy-start
  105.2 2.3 %copy.8 = f32[7,8,32,128]{3,2,1,0:T(8,128)} copy(f32[7,8,32,128]{3,2,1,0:T(8,128)} %bitcast.14) | data formatting | bytes 1835008
  107.4 0.0 copy-done
  107.4 0.9 copy.9
  (6 shorter events, 0.1 us)
Async XLA Ops:
  0.7 0.7 copy-start.1
  105.2 2.3 %copy-start = (f32[7,256,128]{2,1,0:T(8,128)S(1)}, f32[7,256,128]{2,1,0:T(8,128)}, u32[]{:S(2)}) copy-start(f32[7,256,128]{2,1,0:T(8,128)} %get-tuple-element.5) | copy-start | bytes 2752516
